TPU v7x, 128 devices: a whole 4x4x4 slice. The times are simulated.
128 devices in a mesh: gx: 16 (over x, z), gy: 8 (over y, core).
Axes of the slice: x: 4, y: 4, z: 4, core: 2. Of those that a mesh axis runs over, the one named last changes fastest.
Arguments:
- swath_bands: bfloat16 [131072, 6, 128], P(('gx', 'gy')), may hold values from 0 to 1
- clear_weight: bfloat16 [131072, 128], P(('gx', 'gy')), may hold values from 0.049804688 to 1
- owners: int32 [131072, 1], P(('gx', 'gy')), may hold values from 0 to 127; in each aligned block of 1024 rows (0 to 1023, 1024 to 2047, ...) at most 12 rows name the same one
- tile_row: int32 [131072], P(('gx', 'gy')), may hold values from 0 to 255
- columns: int32 [131072, 128], P(('gx', 'gy')), may hold values from 0 to 255
- counts: int32 [128], P(('gx', 'gy')), may hold values from 1 to 1024, 98304 in all
- conduct_x: float32 [2048, 4096], P('gy', 'gx'), may hold values from 0.02 to 0.2
- conduct_y: float32 [2048, 4096], P('gy', 'gx'), may hold values from 0.02 to 0.2
Outputs:
- gridded: float32 [6, 2048, 4096], P(None, 'gy', 'gx')
- coverage: float32 [2048, 4096], P('gy', 'gx')
Inputs may be any that keep to these rules, and one draw needn't show every extreme that they name: `owners`: within the rows of one device no owner is named by more than 12 blocks, a bound that some block reaches. The counts sum to 98304, and some device's count is 1024.
All inputs are finite; a program needn't handle non-finite values.
Results may differ from a plain program's by a relative error of at most 0.0017.
Values may be sent and summed in bfloat16 or wider, within the bound.
No kernel may reach another device: no remote copies, remote signals or barrier semaphores. Data moves between devices by JAX's collectives and lax.ppermute only.
A program may use at most 64 MiB of HBM per device.

v0:
```python
import math

import jax
import jax.numpy as jnp
from jax import lax
from jax.sharding import PartitionSpec as P

floor_weight = 0.15


def padded_2(block, sides, width):
    for axis, dim in sides:
        count = lax.axis_size(axis)
        forward = [(i, i + 1) for i in range(count - 1)]
        backward = [(target, source) for source, target in forward]
        low = lax.ppermute(
            lax.slice_in_dim(block, block.shape[dim] - width, None, axis=dim), axis, forward
        )
        high = lax.ppermute(lax.slice_in_dim(block, 0, width, axis=dim), axis, backward)
        block = jnp.concatenate([low, block, high], axis=dim)
    return block


def smooth_once(current, padded, along_x, along_y):
    east_west = padded[:, 1:-1, 2:] + padded[:, 1:-1, :-2] - 2.0 * current
    north_south = padded[:, 2:, 1:-1] + padded[:, :-2, 1:-1] - 2.0 * current
    return current + along_x[None] * east_west + along_y[None] * north_south


def bin_group(tile_sums, piece_list):
    message_payload, pixel_cols, row_ids = piece_list
    tile_height = tile_sums.shape[0]
    tile_width = tile_sums.shape[2]
    onehot_matrix = (
        pixel_cols[:, :, None] == jnp.arange(tile_width, dtype=jnp.int32)[None, None, :]
    ).astype(jnp.bfloat16)
    binned_values = jnp.einsum(
        "ayn,anq->ayq", message_payload, onehot_matrix, preferred_element_type=jnp.float32
    )
    high_part = binned_values.astype(jnp.bfloat16)
    high_again = lax.optimization_barrier(high_part).astype(jnp.float32)
    low_part = (binned_values - high_again).astype(jnp.bfloat16)
    row_table = (row_ids[:, None] == jnp.arange(tile_height, dtype=jnp.int32)[None, :]).astype(
        jnp.bfloat16
    )
    added = jnp.einsum("ar,ayq->ryq", row_table, high_part, preferred_element_type=jnp.float32)
    added = added + jnp.einsum(
        "ar,ayq->ryq", row_table, low_part, preferred_element_type=jnp.float32
    )
    return (tile_sums + added, None)


def body(swath_bands, clear_weight, owners, tile_row, columns, counts, conduct_x, conduct_y):
    block_slots = swath_bands.shape[0]
    channels = swath_bands.shape[1] + 1
    pixels = swath_bands.shape[2]
    tile_rows, tile_cols = conduct_x.shape
    across = lax.axis_size("gx")
    rows_axis = lax.axis_size("gy")
    devices = across * rows_axis
    capacity = max(2, 3 * block_slots // (2 * devices))
    slot_total = devices * capacity
    position = jnp.arange(block_slots, dtype=jnp.int32)
    is_live = (position < counts[0]).astype(jnp.float32)
    pixel_weight = clear_weight.astype(jnp.float32) * is_live[:, None]
    weighted_bands = (swath_bands.astype(jnp.float32) * pixel_weight[:, None, :]).astype(
        jnp.bfloat16
    )
    weighted = jnp.concatenate(
        [weighted_bands, pixel_weight.astype(jnp.bfloat16)[:, None, :]], axis=1
    )
    target = owners[:, 0]
    same_owner = target[:, None] == target[None, :]
    before = position[None, :] < position[:, None]
    previous_result = jnp.sum(same_owner & before, axis=1)
    slot_of = target * capacity + previous_result
    slot_table = slot_of[None, :] == jnp.arange(slot_total, dtype=jnp.int32)[:, None]
    packed = jnp.dot(
        slot_table.astype(jnp.bfloat16),
        weighted.reshape(block_slots, channels * pixels),
        preferred_element_type=jnp.float32,
    )
    send_data = packed.astype(jnp.bfloat16).reshape(slot_total, channels, pixels)
    index_values = jnp.concatenate(
        [columns.astype(jnp.float32), tile_row.astype(jnp.float32)[:, None]], axis=1
    )
    packed_index = jnp.dot(
        slot_table.astype(jnp.float32),
        index_values,
        precision=lax.Precision.HIGHEST,
        preferred_element_type=jnp.float32,
    )
    packed_index = (packed_index + 0.25).astype(jnp.int32)
    outgoing_columns = packed_index[:, :pixels]
    send_rows = packed_index[:, pixels]
    arrived = (
        lax.all_to_all(
            send_data.reshape(devices, capacity, channels, pixels),
            ("gx", "gy"),
            split_axis=0,
            concat_axis=0,
            tiled=True,
        ),
        lax.all_to_all(
            outgoing_columns.reshape(devices, capacity, pixels),
            ("gx", "gy"),
            split_axis=0,
            concat_axis=0,
            tiled=True,
        ),
        lax.all_to_all(
            send_rows.reshape(devices, capacity),
            ("gx", "gy"),
            split_axis=0,
            concat_axis=0,
            tiled=True,
        ),
    )
    group_size = math.gcd(slot_total, 64)
    group_count = slot_total // group_size
    received_data = arrived[0].reshape(group_count, group_size, channels, pixels)
    recv_cols = arrived[1].reshape(group_count, group_size, pixels)
    recv_rows = arrived[2].reshape(group_count, group_size)
    start_sums = jnp.zeros((tile_rows, channels, tile_cols), jnp.float32)
    tile_sums, unused = lax.scan(bin_group, start_sums, (received_data, recv_cols, recv_rows))
    fields = jnp.transpose(tile_sums, (1, 0, 2))
    for step_index in range(2):
        padded = padded_2(fields, (("gx", 2), ("gy", 1)), 1)
        fields = smooth_once(fields, padded, conduct_x, conduct_y)
    coverage = fields[channels - 1]
    gridded = fields[: channels - 1] / jnp.maximum(coverage, floor_weight)[None]
    return (gridded, coverage)


def solution(mesh):
    return jax.shard_map(
        body,
        mesh=mesh,
        in_specs=(
            P(("gx", "gy"), None, None),
            P(("gx", "gy"), None),
            P(("gx", "gy"), None),
            P(("gx", "gy")),
            P(("gx", "gy"), None),
            P(("gx", "gy")),
            P("gy", "gx"),
            P("gy", "gx"),
        ),
        out_specs=(P(None, "gy", "gx"), P("gy", "gx")),
        check_vma=False,
    )
```

profile of v0, /device:TPU:10, one launch (start us, length us, event | category | flops | bytes accessed | tf_op | source)
XLA Modules:
  0.0 318.9 jit_solution(14080137573345160488)
XLA Ops:
  4.6 3.6 %fusion.21 = s32[1536,129]{0,1:T(8,128)S(1)} fusion(s32[1024]{0:T(1024)S(1)} %multiply_add_fusion, f32[1024,1]{1,0:T(8,128)S(1)} %copy.53, f32[1024,128]{1,0:T(8,128)S(1)} %convert_element_type.48), kind=kOutput, calls=%fused_computation.29 | convolution fusion | flops 2436894720 | bytes 1325056 | tf_op jit(solution)/shard_map/dot_general | solution.py:87
  9.0 10.4 %all-to-all-start = ((s32[128,1,12]{2,1,0:T(1,128)}), s32[128,1,12]{2,1,0:T(1,128)S(1)}, u32[]{:S(2)}, u32[]{:S(2)}) async-start(s32[128,1,12]{2,1,0:T(1,128)} %bitcast.2), calls=%async_computation | async-start | bytes 131072 | tf_op jit(solution)/shard_map/all_to_all | solution.py:111
  24.3 3.0 all-to-all-done
  27.2 6.8 %all-to-all-start.2 = ((s32[128,12,128]{2,1,0:T(8,128)}), s32[128,12,128]{2,1,0:T(8,128)S(1)}, u32[]{:S(2)}, u32[]{:S(2)}) async-start(s32[128,12,128]{2,1,0:T(8,128)} %reshape.47), calls=%async_computation.2 | async-start | bytes 2097152 | tf_op jit(solution)/shard_map/all_to_all | solution.py:104
  35.2 4.8 %fusion.17 = bf16[1536,896]{1,0:T(8,128)(2,1)} fusion(bf16[1024,896]{0,1:T(8,128)(2,1)S(1)} %bitcast.41, s32[1024]{0:T(1024)S(1)} %multiply_add_fusion), kind=kOutput, calls=%fused_computation.24 | convolution fusion | flops 2821521408 | bytes 4591616 | tf_op jit(solution)/shard_map/dot_general | solution.py:78
  40.0 6.3 %reshape_reshape.3 = bf16[128,12,7,128]{3,2,1,0:T(8,128)(2,1)} reshape(bf16[1536,896]{1,0:T(8,128)(2,1)} %fusion.17) | data formatting | bytes 5505024 | tf_op jit(solution)/shard_map/reshape;reshape | solution.py:98
  46.3 4.5 %all-to-all-done.2 = s32[128,12,128]{2,1,0:T(8,128)S(1)} async-done(((s32[128,12,128]{2,1,0:T(8,128)}), s32[128,12,128]{2,1,0:T(8,128)S(1)}, u32[]{:S(2)}, u32[]{:S(2)}) %all-to-all-start.2) | async-done | bytes 786464 | tf_op jit(solution)/shard_map/all_to_all | solution.py:104
  50.7 8.1 %all-to-all-start.1 = ((bf16[128,12,7,128]{3,2,1,0:T(8,128)(2,1)}), bf16[128,12,7,128]{3,2,1,0:T(8,128)(2,1)}, u32[]{:S(2)}, u32[]{:S(2)}) async-start(bf16[128,12,7,128]{3,2,1,0:T(8,128)(2,1)} %reshape_reshape.3), calls=%async_computation.1 | async-start | bytes 6291456 | tf_op jit(solution)/shard_map/all_to_all | solution.py:97
  60.4 37.6 %all-to-all-done.1 = bf16[128,12,7,128]{3,2,1,0:T(8,128)(2,1)} async-done(((bf16[128,12,7,128]{3,2,1,0:T(8,128)(2,1)}), bf16[128,12,7,128]{3,2,1,0:T(8,128)(2,1)}, u32[]{:S(2)}, u32[]{:S(2)}) %all-to-all-start.1) | async-done | bytes 2752544 | tf_op jit(solution)/shard_map/all_to_all | solution.py:97
  97.9 163.6 %while.11 = (s32[]{:T(128)}, f32[256,7,256]{2,0,1:T(8,128)}, s32[24,64]{1,0:T(8,128)S(1)}, bf16[24,64,7,128]{3,2,1,0:T(8,128)(2,1)}, s32[24,64,128]{2,1,0:T(8,128)S(1)}, /*index=5*/s32[]{:T(128)}, s32[]{:T(128)}) while((s32[]{:T(128)}, f32[256,7,256]{2,0,1:T(8,128)}, s32[24,64]{1,0:T(8,128)S(1)}, ...), condition=%wide.region_2.3_spmd.clone, body=%wide.region_1.2_spmd.clone.sunk | while | flops 150765568 | bytes 9635423 | solution.py:125
  97.9 3.0 fusion.60
  103.3 3.0 fusion.60
  106.9 3.3 %select_add_fusion.2 = f32[256,7,256]{2,0,1:T(8,128)} fusion(f32[256,7,256]{2,0,1:T(8,128)} %get-tuple-element.121, f32[256,7,256]{2,0,1:T(8,128)S(1)} %fusion.62, pred[]{:T(512)S(6)} %compare.3, bf16[64,7,256]{2,1,0:T(8,128)(2,1)S(1)} %subtract_convert_fusion.2, s32[64]{0:T(128)S(1)} %fusion.61), kind=kOutput, calls=%fused_computation.3.clone.1 | convolution fusion | flops 60112896 | bytes 5734657 | tf_op jit(solution)/shard_map/while/body/eval_jaxpr/ar,ayq->ryq/dot_general | solution.py:47
  110.2 3.0 fusion.60
  113.8 3.3 %select_add_fusion.2 = f32[256,7,256]{2,0,1:T(8,128)} fusion(f32[256,7,256]{2,0,1:T(8,128)} %get-tuple-element.121, f32[256,7,256]{2,0,1:T(8,128)S(1)} %fusion.62, pred[]{:T(512)S(6)} %compare.3, bf16[64,7,256]{2,1,0:T(8,128)(2,1)S(1)} %subtract_convert_fusion.2, s32[64]{0:T(128)S(1)} %fusion.61), kind=kOutput, calls=%fused_computation.3.clone.1 | convolution fusion | flops 60112896 | bytes 5734657 | tf_op jit(solution)/shard_map/while/body/eval_jaxpr/ar,ayq->ryq/dot_general | solution.py:47
  117.1 3.0 fusion.60
  120.7 3.3 %select_add_fusion.2 = f32[256,7,256]{2,0,1:T(8,128)} fusion(f32[256,7,256]{2,0,1:T(8,128)} %get-tuple-element.121, f32[256,7,256]{2,0,1:T(8,128)S(1)} %fusion.62, pred[]{:T(512)S(6)} %compare.3, bf16[64,7,256]{2,1,0:T(8,128)(2,1)S(1)} %subtract_convert_fusion.2, s32[64]{0:T(128)S(1)} %fusion.61), kind=kOutput, calls=%fused_computation.3.clone.1 | convolution fusion | flops 60112896 | bytes 5734657 | tf_op jit(solution)/shard_map/while/body/eval_jaxpr/ar,ayq->ryq/dot_general | solution.py:47
  124.0 3.0 fusion.60
  127.6 3.3 %select_add_fusion.2 = f32[256,7,256]{2,0,1:T(8,128)} fusion(f32[256,7,256]{2,0,1:T(8,128)} %get-tuple-element.121, f32[256,7,256]{2,0,1:T(8,128)S(1)} %fusion.62, pred[]{:T(512)S(6)} %compare.3, bf16[64,7,256]{2,1,0:T(8,128)(2,1)S(1)} %subtract_convert_fusion.2, s32[64]{0:T(128)S(1)} %fusion.61), kind=kOutput, calls=%fused_computation.3.clone.1 | convolution fusion | flops 60112896 | bytes 5734657 | tf_op jit(solution)/shard_map/while/body/eval_jaxpr/ar,ayq->ryq/dot_general | solution.py:47
  130.9 3.0 fusion.60
  134.5 3.3 %select_add_fusion.2 = f32[256,7,256]{2,0,1:T(8,128)} fusion(f32[256,7,256]{2,0,1:T(8,128)} %get-tuple-element.121, f32[256,7,256]{2,0,1:T(8,128)S(1)} %fusion.62, pred[]{:T(512)S(6)} %compare.3, bf16[64,7,256]{2,1,0:T(8,128)(2,1)S(1)} %subtract_convert_fusion.2, s32[64]{0:T(128)S(1)} %fusion.61), kind=kOutput, calls=%fused_computation.3.clone.1 | convolution fusion | flops 60112896 | bytes 5734657 | tf_op jit(solution)/shard_map/while/body/eval_jaxpr/ar,ayq->ryq/dot_general | solution.py:47
  137.7 3.0 fusion.60
  141.3 3.3 %select_add_fusion.2 = f32[256,7,256]{2,0,1:T(8,128)} fusion(f32[256,7,256]{2,0,1:T(8,128)} %get-tuple-element.121, f32[256,7,256]{2,0,1:T(8,128)S(1)} %fusion.62, pred[]{:T(512)S(6)} %compare.3, bf16[64,7,256]{2,1,0:T(8,128)(2,1)S(1)} %subtract_convert_fusion.2, s32[64]{0:T(128)S(1)} %fusion.61), kind=kOutput, calls=%fused_computation.3.clone.1 | convolution fusion | flops 60112896 | bytes 5734657 | tf_op jit(solution)/shard_map/while/body/eval_jaxpr/ar,ayq->ryq/dot_general | solution.py:47
  144.6 3.0 fusion.60
  148.2 3.3 %select_add_fusion.2 = f32[256,7,256]{2,0,1:T(8,128)} fusion(f32[256,7,256]{2,0,1:T(8,128)} %get-tuple-element.121, f32[256,7,256]{2,0,1:T(8,128)S(1)} %fusion.62, pred[]{:T(512)S(6)} %compare.3, bf16[64,7,256]{2,1,0:T(8,128)(2,1)S(1)} %subtract_convert_fusion.2, s32[64]{0:T(128)S(1)} %fusion.61), kind=kOutput, calls=%fused_computation.3.clone.1 | convolution fusion | flops 60112896 | bytes 5734657 | tf_op jit(solution)/shard_map/while/body/eval_jaxpr/ar,ayq->ryq/dot_general | solution.py:47
  151.5 3.0 fusion.60
  155.1 3.3 %select_add_fusion.2 = f32[256,7,256]{2,0,1:T(8,128)} fusion(f32[256,7,256]{2,0,1:T(8,128)} %get-tuple-element.121, f32[256,7,256]{2,0,1:T(8,128)S(1)} %fusion.62, pred[]{:T(512)S(6)} %compare.3, bf16[64,7,256]{2,1,0:T(8,128)(2,1)S(1)} %subtract_convert_fusion.2, s32[64]{0:T(128)S(1)} %fusion.61), kind=kOutput, calls=%fused_computation.3.clone.1 | convolution fusion | flops 60112896 | bytes 5734657 | tf_op jit(solution)/shard_map/while/body/eval_jaxpr/ar,ayq->ryq/dot_general | solution.py:47
  158.4 3.0 fusion.60
  162.0 3.3 %select_add_fusion.2 = f32[256,7,256]{2,0,1:T(8,128)} fusion(f32[256,7,256]{2,0,1:T(8,128)} %get-tuple-element.121, f32[256,7,256]{2,0,1:T(8,128)S(1)} %fusion.62, pred[]{:T(512)S(6)} %compare.3, bf16[64,7,256]{2,1,0:T(8,128)(2,1)S(1)} %subtract_convert_fusion.2, s32[64]{0:T(128)S(1)} %fusion.61), kind=kOutput, calls=%fused_computation.3.clone.1 | convolution fusion | flops 60112896 | bytes 5734657 | tf_op jit(solution)/shard_map/while/body/eval_jaxpr/ar,ayq->ryq/dot_general | solution.py:47
  165.3 3.0 fusion.60
  168.9 3.3 %select_add_fusion.2 = f32[256,7,256]{2,0,1:T(8,128)} fusion(f32[256,7,256]{2,0,1:T(8,128)} %get-tuple-element.121, f32[256,7,256]{2,0,1:T(8,128)S(1)} %fusion.62, pred[]{:T(512)S(6)} %compare.3, bf16[64,7,256]{2,1,0:T(8,128)(2,1)S(1)} %subtract_convert_fusion.2, s32[64]{0:T(128)S(1)} %fusion.61), kind=kOutput, calls=%fused_computation.3.clone.1 | convolution fusion | flops 60112896 | bytes 5734657 | tf_op jit(solution)/shard_map/while/body/eval_jaxpr/ar,ayq->ryq/dot_general | solution.py:47
  172.1 3.0 fusion.60
  175.7 3.3 %select_add_fusion.2 = f32[256,7,256]{2,0,1:T(8,128)} fusion(f32[256,7,256]{2,0,1:T(8,128)} %get-tuple-element.121, f32[256,7,256]{2,0,1:T(8,128)S(1)} %fusion.62, pred[]{:T(512)S(6)} %compare.3, bf16[64,7,256]{2,1,0:T(8,128)(2,1)S(1)} %subtract_convert_fusion.2, s32[64]{0:T(128)S(1)} %fusion.61), kind=kOutput, calls=%fused_computation.3.clone.1 | convolution fusion | flops 60112896 | bytes 5734657 | tf_op jit(solution)/shard_map/while/body/eval_jaxpr/ar,ayq->ryq/dot_general | solution.py:47
  179.0 3.0 fusion.60
  182.6 3.3 %select_add_fusion.2 = f32[256,7,256]{2,0,1:T(8,128)} fusion(f32[256,7,256]{2,0,1:T(8,128)} %get-tuple-element.121, f32[256,7,256]{2,0,1:T(8,128)S(1)} %fusion.62, pred[]{:T(512)S(6)} %compare.3, bf16[64,7,256]{2,1,0:T(8,128)(2,1)S(1)} %subtract_convert_fusion.2, s32[64]{0:T(128)S(1)} %fusion.61), kind=kOutput, calls=%fused_computation.3.clone.1 | convolution fusion | flops 60112896 | bytes 5734657 | tf_op jit(solution)/shard_map/while/body/eval_jaxpr/ar,ayq->ryq/dot_general | solution.py:47
  185.9 3.0 fusion.60
  189.5 3.3 %select_add_fusion.2 = f32[256,7,256]{2,0,1:T(8,128)} fusion(f32[256,7,256]{2,0,1:T(8,128)} %get-tuple-element.121, f32[256,7,256]{2,0,1:T(8,128)S(1)} %fusion.62, pred[]{:T(512)S(6)} %compare.3, bf16[64,7,256]{2,1,0:T(8,128)(2,1)S(1)} %subtract_convert_fusion.2, s32[64]{0:T(128)S(1)} %fusion.61), kind=kOutput, calls=%fused_computation.3.clone.1 | convolution fusion | flops 60112896 | bytes 5734657 | tf_op jit(solution)/shard_map/while/body/eval_jaxpr/ar,ayq->ryq/dot_general | solution.py:47
  192.8 3.0 fusion.60
  196.4 3.3 %select_add_fusion.2 = f32[256,7,256]{2,0,1:T(8,128)} fusion(f32[256,7,256]{2,0,1:T(8,128)} %get-tuple-element.121, f32[256,7,256]{2,0,1:T(8,128)S(1)} %fusion.62, pred[]{:T(512)S(6)} %compare.3, bf16[64,7,256]{2,1,0:T(8,128)(2,1)S(1)} %subtract_convert_fusion.2, s32[64]{0:T(128)S(1)} %fusion.61), kind=kOutput, calls=%fused_computation.3.clone.1 | convolution fusion | flops 60112896 | bytes 5734657 | tf_op jit(solution)/shard_map/while/body/eval_jaxpr/ar,ayq->ryq/dot_general | solution.py:47
  199.7 3.0 fusion.60
  203.3 3.3 %select_add_fusion.2 = f32[256,7,256]{2,0,1:T(8,128)} fusion(f32[256,7,256]{2,0,1:T(8,128)} %get-tuple-element.121, f32[256,7,256]{2,0,1:T(8,128)S(1)} %fusion.62, pred[]{:T(512)S(6)} %compare.3, bf16[64,7,256]{2,1,0:T(8,128)(2,1)S(1)} %subtract_convert_fusion.2, s32[64]{0:T(128)S(1)} %fusion.61), kind=kOutput, calls=%fused_computation.3.clone.1 | convolution fusion | flops 60112896 | bytes 5734657 | tf_op jit(solution)/shard_map/while/body/eval_jaxpr/ar,ayq->ryq/dot_general | solution.py:47
  206.5 3.0 fusion.60
  210.1 3.3 %select_add_fusion.2 = f32[256,7,256]{2,0,1:T(8,128)} fusion(f32[256,7,256]{2,0,1:T(8,128)} %get-tuple-element.121, f32[256,7,256]{2,0,1:T(8,128)S(1)} %fusion.62, pred[]{:T(512)S(6)} %compare.3, bf16[64,7,256]{2,1,0:T(8,128)(2,1)S(1)} %subtract_convert_fusion.2, s32[64]{0:T(128)S(1)} %fusion.61), kind=kOutput, calls=%fused_computation.3.clone.1 | convolution fusion | flops 60112896 | bytes 5734657 | tf_op jit(solution)/shard_map/while/body/eval_jaxpr/ar,ayq->ryq/dot_general | solution.py:47
  213.4 3.0 fusion.60
  217.0 3.3 %select_add_fusion.2 = f32[256,7,256]{2,0,1:T(8,128)} fusion(f32[256,7,256]{2,0,1:T(8,128)} %get-tuple-element.121, f32[256,7,256]{2,0,1:T(8,128)S(1)} %fusion.62, pred[]{:T(512)S(6)} %compare.3, bf16[64,7,256]{2,1,0:T(8,128)(2,1)S(1)} %subtract_convert_fusion.2, s32[64]{0:T(128)S(1)} %fusion.61), kind=kOutput, calls=%fused_computation.3.clone.1 | convolution fusion | flops 60112896 | bytes 5734657 | tf_op jit(solution)/shard_map/while/body/eval_jaxpr/ar,ayq->ryq/dot_general | solution.py:47
  220.3 3.0 fusion.60
  223.9 3.3 %select_add_fusion.2 = f32[256,7,256]{2,0,1:T(8,128)} fusion(f32[256,7,256]{2,0,1:T(8,128)} %get-tuple-element.121, f32[256,7,256]{2,0,1:T(8,128)S(1)} %fusion.62, pred[]{:T(512)S(6)} %compare.3, bf16[64,7,256]{2,1,0:T(8,128)(2,1)S(1)} %subtract_convert_fusion.2, s32[64]{0:T(128)S(1)} %fusion.61), kind=kOutput, calls=%fused_computation.3.clone.1 | convolution fusion | flops 60112896 | bytes 5734657 | tf_op jit(solution)/shard_map/while/body/eval_jaxpr/ar,ayq->ryq/dot_general | solution.py:47
  227.2 3.0 fusion.60
  230.8 3.3 %select_add_fusion.2 = f32[256,7,256]{2,0,1:T(8,128)} fusion(f32[256,7,256]{2,0,1:T(8,128)} %get-tuple-element.121, f32[256,7,256]{2,0,1:T(8,128)S(1)} %fusion.62, pred[]{:T(512)S(6)} %compare.3, bf16[64,7,256]{2,1,0:T(8,128)(2,1)S(1)} %subtract_convert_fusion.2, s32[64]{0:T(128)S(1)} %fusion.61), kind=kOutput, calls=%fused_computation.3.clone.1 | convolution fusion | flops 60112896 | bytes 5734657 | tf_op jit(solution)/shard_map/while/body/eval_jaxpr/ar,ayq->ryq/dot_general | solution.py:47
  234.1 3.0 fusion.60
  237.7 3.3 %select_add_fusion.2 = f32[256,7,256]{2,0,1:T(8,128)} fusion(f32[256,7,256]{2,0,1:T(8,128)} %get-tuple-element.121, f32[256,7,256]{2,0,1:T(8,128)S(1)} %fusion.62, pred[]{:T(512)S(6)} %compare.3, bf16[64,7,256]{2,1,0:T(8,128)(2,1)S(1)} %subtract_convert_fusion.2, s32[64]{0:T(128)S(1)} %fusion.61), kind=kOutput, calls=%fused_computation.3.clone.1 | convolution fusion | flops 60112896 | bytes 5734657 | tf_op jit(solution)/shard_map/while/body/eval_jaxpr/ar,ayq->ryq/dot_general | solution.py:47
  240.9 3.0 fusion.60
  244.5 3.3 %select_add_fusion.2 = f32[256,7,256]{2,0,1:T(8,128)} fusion(f32[256,7,256]{2,0,1:T(8,128)} %get-tuple-element.121, f32[256,7,256]{2,0,1:T(8,128)S(1)} %fusion.62, pred[]{:T(512)S(6)} %compare.3, bf16[64,7,256]{2,1,0:T(8,128)(2,1)S(1)} %subtract_convert_fusion.2, s32[64]{0:T(128)S(1)} %fusion.61), kind=kOutput, calls=%fused_computation.3.clone.1 | convolution fusion | flops 60112896 | bytes 5734657 | tf_op jit(solution)/shard_map/while/body/eval_jaxpr/ar,ayq->ryq/dot_general | solution.py:47
  247.8 3.0 fusion.60
  251.4 3.3 %select_add_fusion.2 = f32[256,7,256]{2,0,1:T(8,128)} fusion(f32[256,7,256]{2,0,1:T(8,128)} %get-tuple-element.121, f32[256,7,256]{2,0,1:T(8,128)S(1)} %fusion.62, pred[]{:T(512)S(6)} %compare.3, bf16[64,7,256]{2,1,0:T(8,128)(2,1)S(1)} %subtract_convert_fusion.2, s32[64]{0:T(128)S(1)} %fusion.61), kind=kOutput, calls=%fused_computation.3.clone.1 | convolution fusion | flops 60112896 | bytes 5734657 | tf_op jit(solution)/shard_map/while/body/eval_jaxpr/ar,ayq->ryq/dot_general | solution.py:47
  254.7 3.0 fusion.60
  258.3 3.3 %select_add_fusion.2 = f32[256,7,256]{2,0,1:T(8,128)} fusion(f32[256,7,256]{2,0,1:T(8,128)} %get-tuple-element.121, f32[256,7,256]{2,0,1:T(8,128)S(1)} %fusion.62, pred[]{:T(512)S(6)} %compare.3, bf16[64,7,256]{2,1,0:T(8,128)(2,1)S(1)} %subtract_convert_fusion.2, s32[64]{0:T(128)S(1)} %fusion.61), kind=kOutput, calls=%fused_computation.3.clone.1 | convolution fusion | flops 60112896 | bytes 5734657 | tf_op jit(solution)/shard_map/while/body/eval_jaxpr/ar,ayq->ryq/dot_general | solution.py:47
  263.4 3.2 %collective-permute-start = (f32[7,256,1]{1,2,0:T(1,128)S(1)}, f32[7,256,1]{1,2,0:T(1,128)S(1)}, u32[]{:S(2)}, u32[]{:S(2)}) collective-permute-start(f32[7,256,1]{1,2,0:T(1,128)S(1)} %get-tuple-element.75), channel_id=1, source_target_pairs={{8,0},{16,8},{24,16},{32,24},{40,32},{48,40},{56,48},{64,56},{72,6... | collective-permute-start | bytes 21512 | tf_op jit(solution)/shard_map/ppermute | solution.py:19
  266.6 2.8 collective-permute-start.1
  269.5 4.8 %collective-permute-done.1 = f32[7,256,1]{1,2,0:T(1,128)S(1)} collective-permute-done((f32[7,256,1]{1,2,0:T(1,128)S(1)}, f32[7,256,1]{1,2,0:T(1,128)S(1)}, u32[]{:S(2)}, u32[]{:S(2)}) %collective-permute-start.1) | collective-permute-done | bytes 7200 | tf_op jit(solution)/shard_map/ppermute | solution.py:16
  286.9 3.9 %fusion.33 = f32[7,256,256]{1,2,0:T(8,128)S(1)} fusion(f32[7,1,258]{1,2,0:T(8,128)} %copy.64, f32[7,256,1]{1,2,0:T(1,128)S(1)} %collective-permute-done, f32[7,256,256]{1,2,0:T(8,128)S(1)} %bitcast.40, f32[7,256,1]{1,2,0:T(1,128)S(1)} %collective-permute-done.1, f32[7,1,258]{1,2,0:T(8,128)S(1)} %copy.62, f32[256,256]{0,1:T(8,128)S(1)} %copy.60, ...), kind=kLoop, calls=%fused_computation.52 | loop fusion | flops 7798784 | bytes 4223088 | tf_op jit(solution)/shard_map/add | solution.py:27
  292.8 3.9 %collective-permute-start.5 = (f32[7,256,1]{1,2,0:T(1,128)S(1)}, f32[7,256,1]{1,2,0:T(1,128)S(1)}, u32[]{:S(2)}, u32[]{:S(2)}) collective-permute-start(f32[7,256,1]{1,2,0:T(1,128)S(1)} %get-tuple-element.72), channel_id=1, source_target_pairs={{0,8},{8,16},{16,24},{24,32},{32,40},{40,48},{48,56},{56,64},{64,7... | collective-permute-start | bytes 21512 | tf_op jit(solution)/shard_map/ppermute | solution.py:16
  296.7 3.7 %collective-permute-done.5 = f32[7,256,1]{1,2,0:T(1,128)S(1)} collective-permute-done((f32[7,256,1]{1,2,0:T(1,128)S(1)}, f32[7,256,1]{1,2,0:T(1,128)S(1)}, u32[]{:S(2)}, u32[]{:S(2)}) %collective-permute-start.5) | collective-permute-done | bytes 7200 | tf_op jit(solution)/shard_map/ppermute | solution.py:16
  312.3 3.9 %fusion.25 = f32[7,256,256]{1,2,0:T(8,128)S(1)} fusion(f32[7,1,258]{1,2,0:T(8,128)} %copy.68, f32[7,256,1]{1,2,0:T(1,128)S(1)} %collective-permute-done.4, f32[7,256,256]{1,2,0:T(8,128)S(1)} %copy-done.1, f32[7,256,1]{1,2,0:T(1,128)S(1)} %collective-permute-done.5, f32[7,1,258]{1,2,0:T(8,128)S(1)} %copy.66, f32[256,256]{0,1:T(8,128)S(1)} %copy.60, ...), kind=kLoop, calls=%fused_computation.36 | loop fusion | flops 7798784 | bytes 4223088 | tf_op jit(solution)/shard_map/add | solution.py:27
  (162 shorter events, 58.0 us)
Async XLA Ops:
  4.6 14.8 %copy-start.4 = (bf16[1024,128]{1,0:T(8,128)(2,1)S(1)}, bf16[1024,128]{1,0:T(8,128)(2,1)}, u32[]{:S(2)}) copy-start(bf16[1024,128]{1,0:T(8,128)(2,1)} %param.11) | copy-start | bytes 786436
  9.0 18.2 %all-to-all-start = ((s32[128,1,12]{2,1,0:T(1,128)}), s32[128,1,12]{2,1,0:T(1,128)S(1)}, u32[]{:S(2)}, u32[]{:S(2)}) async-start(s32[128,1,12]{2,1,0:T(1,128)} %bitcast.2), calls=%async_computation | async-start | bytes 131072 | tf_op jit(solution)/shard_map/all_to_all | solution.py:111
  23.2 10.8 %copy-start.2 = (f32[1024,128]{0,1:T(8,128)S(1)}, f32[1024,128]{0,1:T(8,128)}, u32[]{:S(2)}) copy-start(f32[1024,128]{0,1:T(8,128)} %get-tuple-element.76) | copy-start | bytes 1572868
  27.2 23.5 %all-to-all-start.2 = ((s32[128,12,128]{2,1,0:T(8,128)}), s32[128,12,128]{2,1,0:T(8,128)S(1)}, u32[]{:S(2)}, u32[]{:S(2)}) async-start(s32[128,12,128]{2,1,0:T(8,128)} %reshape.47), calls=%async_computation.2 | async-start | bytes 2097152 | tf_op jit(solution)/shard_map/all_to_all | solution.py:104
  34.1 1.0 copy-start.3
  50.7 47.2 %all-to-all-start.1 = ((bf16[128,12,7,128]{3,2,1,0:T(8,128)(2,1)}), bf16[128,12,7,128]{3,2,1,0:T(8,128)(2,1)}, u32[]{:S(2)}, u32[]{:S(2)}) async-start(bf16[128,12,7,128]{3,2,1,0:T(8,128)(2,1)} %reshape_reshape.3), calls=%async_computation.1 | async-start | bytes 6291456 | tf_op jit(solution)/shard_map/all_to_all | solution.py:97
  263.4 6.0 %collective-permute-start = (f32[7,256,1]{1,2,0:T(1,128)S(1)}, f32[7,256,1]{1,2,0:T(1,128)S(1)}, u32[]{:S(2)}, u32[]{:S(2)}) collective-permute-start(f32[7,256,1]{1,2,0:T(1,128)S(1)} %get-tuple-element.75), channel_id=1, source_target_pairs={{8,0},{16,8},{24,16},{32,24},{40,32},{48,40},{56,48},{64,56},{72,6... | collective-permute-start | bytes 21512 | tf_op jit(solution)/shard_map/ppermute | solution.py:19
  266.6 7.6 %collective-permute-start.1 = (f32[7,256,1]{1,2,0:T(1,128)S(1)}, f32[7,256,1]{1,2,0:T(1,128)S(1)}, u32[]{:S(2)}, u32[]{:S(2)}) collective-permute-start(f32[7,256,1]{1,2,0:T(1,128)S(1)} %get-tuple-element.74), channel_id=1, source_target_pairs={{0,8},{8,16},{16,24},{24,32},{32,40},{40,48},{48,56},{56,64},{64,7... | collective-permute-start | bytes 21512 | tf_op jit(solution)/shard_map/ppermute | solution.py:16
  275.6 6.4 %copy-start.5 = (f32[256,256]{1,0:T(8,128)S(1)}, f32[256,256]{1,0:T(8,128)}, u32[]{:S(2)}) copy-start(f32[256,256]{1,0:T(8,128)} %param.16) | copy-start | bytes 786436
  277.3 6.0 %collective-permute-start.2 = (f32[7,1,258]{2,1,0:T(1,128)S(1)}, f32[7,1,258]{2,1,0:T(1,128)S(1)}, u32[]{:S(2)}, u32[]{:S(2)}) collective-permute-start(f32[7,1,258]{2,1,0:T(1,128)S(1)} %copy.61), channel_id=1, source_target_pairs={{1,0},{2,1},{3,2},{4,3},{5,4},{6,5},{7,6},{9,8},{10,9},{11,10},{12... | collective-permute-start | bytes 21680 | tf_op jit(solution)/shard_map/ppermute | solution.py:19
  280.0 5.6 %collective-permute-start.3 = (f32[7,1,258]{2,1,0:T(1,128)S(1)}, f32[7,1,258]{2,1,0:T(1,128)S(1)}, u32[]{:S(2)}, u32[]{:S(2)}) collective-permute-start(f32[7,1,258]{2,1,0:T(1,128)S(1)} %copy.63), channel_id=1, source_target_pairs={{0,1},{1,2},{2,3},{3,4},{4,5},{5,6},{6,7},{8,9},{9,10},{10,11},{11... | collective-permute-start | bytes 21680 | tf_op jit(solution)/shard_map/ppermute | solution.py:16
  290.8 9.8 %copy-start = (f32[7,256,256]{1,2,0:T(8,128)}, f32[7,256,256]{1,2,0:T(8,128)S(1)}, u32[]{:S(2)}) copy-start(f32[7,256,256]{1,2,0:T(8,128)S(1)} %fusion.33) | copy-start | bytes 5505028
  290.9 5.9 %collective-permute-start.4 = (f32[7,256,1]{1,2,0:T(1,128)S(1)}, f32[7,256,1]{1,2,0:T(1,128)S(1)}, u32[]{:S(2)}, u32[]{:S(2)}) collective-permute-start(f32[7,256,1]{1,2,0:T(1,128)S(1)} %get-tuple-element.73), channel_id=1, source_target_pairs={{8,0},{16,8},{24,16},{32,24},{40,32},{48,40},{56,48},{64,56},{72,6... | collective-permute-start | bytes 21512 | tf_op jit(solution)/shard_map/ppermute | solution.py:19
  292.8 7.6 %collective-permute-start.5 = (f32[7,256,1]{1,2,0:T(1,128)S(1)}, f32[7,256,1]{1,2,0:T(1,128)S(1)}, u32[]{:S(2)}, u32[]{:S(2)}) collective-permute-start(f32[7,256,1]{1,2,0:T(1,128)S(1)} %get-tuple-element.72), channel_id=1, source_target_pairs={{0,8},{8,16},{16,24},{24,32},{32,40},{40,48},{48,56},{56,64},{64,7... | collective-permute-start | bytes 21512 | tf_op jit(solution)/shard_map/ppermute | solution.py:16
  301.9 10.4 %copy-start.1 = (f32[7,256,256]{1,2,0:T(8,128)S(1)}, f32[7,256,256]{1,2,0:T(8,128)}, u32[]{:S(2)}) copy-start(f32[7,256,256]{1,2,0:T(8,128)} %copy-done) | copy-start | bytes 5505028
  303.6 4.8 %collective-permute-start.6 = (f32[7,1,258]{2,1,0:T(1,128)S(1)}, f32[7,1,258]{2,1,0:T(1,128)S(1)}, u32[]{:S(2)}, u32[]{:S(2)}) collective-permute-start(f32[7,1,258]{2,1,0:T(1,128)S(1)} %copy.65), channel_id=1, source_target_pairs={{1,0},{2,1},{3,2},{4,3},{5,4},{6,5},{7,6},{9,8},{10,9},{11,10},{12... | collective-permute-start | bytes 21680 | tf_op jit(solution)/shard_map/ppermute | solution.py:19
  306.0 5.0 %collective-permute-start.7 = (f32[7,1,258]{2,1,0:T(1,128)S(1)}, f32[7,1,258]{2,1,0:T(1,128)S(1)}, u32[]{:S(2)}, u32[]{:S(2)}) collective-permute-start(f32[7,1,258]{2,1,0:T(1,128)S(1)} %copy.67), channel_id=1, source_target_pairs={{0,1},{1,2},{2,3},{3,4},{4,5},{5,6},{6,7},{8,9},{9,10},{10,11},{11... | collective-permute-start | bytes 21680 | tf_op jit(solution)/shard_map/ppermute | solution.py:16
where the time goes:
time: 325 us; the launch traced here: 319 us
  matrix products  170 us (52%)
  waiting for transfers between devices  57.7 us (18%)
  starting transfers between devices  45.9 us (14%)
  local copies, waits for them, and re-layouts  27.5 us (8%)
  other arithmetic  15.9 us (5%)
    dot_general x24, matrix products, bin_group(): jnp.einsum('ar,ayq->ryq', row_table, low_part, preferred_element_type=jnp...  77.1 us
    dot_general x24, matrix products, bin_group(): jnp.einsum('ayn,anq->ayq', message_payload, onehot_matrix, preferred_elem...  71.9 us
    all_to_all x1, waiting for transfers between devices, body(): lax.all_to_all(send_data.reshape(devices, capacity, channels, pixels), ('...  37.6 us
    ppermute x4, waiting for transfers between devices, padded_2(): lax.ppermute(lax.slice_in_dim(block, block.shape[dim] - width, None, axis...  12.6 us
    dot_general x24, matrix products, bin_group(): jnp.einsum('ar,ayq->ryq', row_table, high_part, preferred_element_type=jn...  12.3 us
    ppermute x4, starting transfers between devices, padded_2(): lax.ppermute(lax.slice_in_dim(block, block.shape[dim] - width, None, axis...  11.2 us
    all_to_all x1, starting transfers between devices, body(): lax.all_to_all(send_rows.reshape(devices, capacity), ('gx', 'gy'), split_...  10.4 us
    ppermute x4, starting transfers between devices, padded_2(): lax.ppermute(lax.slice_in_dim(block, 0, width, axis=dim), axis, backward)  9.34 us
  transfers between devices with their start and end apart: 11, of which 7 were waited for; matrix products, arithmetic and copies ran while one was open for 6% of the time, Pallas kernels for 0%

commit v1 on v0

v1 whole, which is shorter than its diff:
```python
import functools

import jax
import jax.numpy as jnp
from jax import lax
from jax.experimental import pallas as pl
from jax.experimental.pallas import tpu as pltpu
from jax.sharding import PartitionSpec as P

CAPACITY = 12
SLOTS = CAPACITY + 1
FLOOR = 0.15
HALO = 2

f32 = jnp.float32
bf16 = jnp.bfloat16
i32 = jnp.int32


def iota(shape, dim):
    return lax.broadcasted_iota(i32, shape, dim)


def ring(count, step):
    return [(i, (i + step) % count) for i in range(count)]


def pack_kernel(
    count_ref,
    owner_ref,
    row_ref,
    swath_ref,
    weight_ref,
    cols_ref,
    out_ref,
    weight_f,
    cols_f,
    codes_f,
    slot_v,
    slot_s,
    sem,
):
    blocks = swath_ref.shape[0]
    devices = out_ref.shape[0] // SLOTS
    live_count = count_ref[0]
    owner = owner_ref[...]
    live = iota((1, blocks), 1) < live_count
    owner = jnp.where(live, owner, -1)
    named = (iota((devices, blocks), 0) == owner).astype(f32)
    named16 = named.astype(bf16)
    earlier = (iota((blocks, blocks), 0) < iota((blocks, blocks), 1)).astype(f32).astype(bf16)
    before = jnp.dot(named16, earlier, preferred_element_type=f32)
    rank = jnp.sum(named * before, axis=0, keepdims=True).astype(i32)
    slot_v[...] = jnp.where(live, owner * SLOTS + rank, CAPACITY)
    copy = pltpu.make_async_copy(slot_v, slot_s, sem)
    copy.start()
    place = jnp.where(
        iota((128, blocks), 0) == rank, (row_ref[...] + 1).astype(f32), 0.0
    ).astype(bf16)
    codes_f[...] = lax.dot_general(
        named16, place, (((1,), (1,)), ((), ())), preferred_element_type=f32
    )
    weight_f[...] = weight_ref[...].astype(f32)
    cols_f[...] = cols_ref[...].astype(f32)

    @pl.loop(0, devices)
    def _(t):
        out_ref[pl.ds(t * SLOTS, SLOTS)] = jnp.zeros((SLOTS, 8, 128), bf16)

    copy.wait()

    @pl.loop(0, (live_count + 7) // 8)
    def _(group):
        for i in range(8):
            b = group * 8 + i
            slot = slot_s[0, b]
            w = weight_f[pl.ds(b, 1), :]
            c = cols_f[pl.ds(b, 1), :]
            bands = swath_ref[b].astype(f32) * w
            out_ref[slot] = jnp.concatenate([bands, w, c], axis=0).astype(bf16)

    @pl.loop(0, devices, unroll=4)
    def _(t):
        code = codes_f[pl.ds(t, 1), :]
        out_ref[t * SLOTS + CAPACITY] = jnp.broadcast_to(code, (8, 128)).astype(bf16)


def pack(counts, owners, tile_row, swath, weight, columns, devices):
    blocks = swath.shape[0]
    vmem = pl.BlockSpec(memory_space=pltpu.VMEM)
    return pl.pallas_call(
        pack_kernel,
        out_shape=jax.ShapeDtypeStruct((devices * SLOTS, 8, 128), bf16),
        in_specs=[pl.BlockSpec(memory_space=pltpu.SMEM)] + [vmem] * 5,
        out_specs=vmem,
        scratch_shapes=[
            pltpu.VMEM((blocks, 128), f32),
            pltpu.VMEM((blocks, 128), f32),
            pltpu.VMEM((devices, 128), f32),
            pltpu.VMEM((1, blocks), i32),
            pltpu.SMEM((1, blocks), i32),
            pltpu.SemaphoreType.DMA,
        ],
        compiler_params=pltpu.CompilerParams(vmem_limit_bytes=48 << 20),
        name="pack",
    )(counts, owners, tile_row, swath, weight, columns)


def bin_kernel(
    msg_ref, acc_ref, top_ref, bottom_ref, left_ref, right_ref, codes_v, codes_s, sem
):
    sources = msg_ref.shape[0] // SLOTS
    height, _, width = acc_ref.shape

    @pl.loop(0, sources, unroll=4)
    def _(s):
        tile = msg_ref[s * SLOTS + CAPACITY].astype(f32)
        codes_v[pl.ds(s, 1), :] = tile[0:1, :].astype(i32)

    copy = pltpu.make_async_copy(codes_v, codes_s, sem)
    copy.start()

    @pl.loop(0, height // 8)
    def _(g):
        acc_ref[pl.ds(g * 8, 8)] = jnp.zeros((8, 8, width), f32)

    copy.wait()
    lanes = iota((width, 128), 0).astype(f32).astype(bf16)
    one = jnp.ones((width, 128), bf16)
    zero = jnp.zeros((width, 128), bf16)
    empty = jnp.zeros((8, 128), bf16)

    @pl.loop(0, sources)
    def _(s):
        for k in range(0, CAPACITY, 2):
            first = msg_ref[s * SLOTS + k]
            second = msg_ref[s * SLOTS + k + 1]
            hits = jnp.concatenate(
                [
                    jnp.where(lanes == first[7:8, :], one, zero),
                    jnp.where(lanes == second[7:8, :], one, zero),
                ],
                axis=1,
            )
            values = jnp.concatenate(
                [
                    jnp.concatenate([first, empty], axis=1),
                    jnp.concatenate([empty, second], axis=1),
                ],
                axis=0,
            )
            sums = lax.dot_general(
                values, hits, (((1,), (1,)), ((), ())), preferred_element_type=f32
            )
            for j in range(2):
                row = jnp.maximum(codes_s[s, k + j] - 1, 0)
                acc_ref[row] += sums[8 * j : 8 * j + 8]

    top_ref[...] = acc_ref[0:HALO]
    bottom_ref[...] = acc_ref[height - HALO : height]
    lane = iota((8, 128), 1)
    blank = jnp.zeros((8, 128), f32)

    def edges(j, carry):
        here = lane // 2 == j
        result = []
        for q in range(4):
            near = pltpu.roll(acc_ref[q * 64 + j, :, 0:128], 2 * j, 1)
            result.append(jnp.where(here, near, carry[2 * q]))
            far = pltpu.roll(acc_ref[q * 64 + j, :, width - 128 : width], 2 * j + 2, 1)
            result.append(jnp.where(here, far, carry[2 * q + 1]))
        return tuple(result)

    strips = lax.fori_loop(0, 64, edges, (blank,) * 8)
    for q in range(4):
        left_ref[q] = strips[2 * q]
        right_ref[q] = strips[2 * q + 1]


def bin_blocks(message, height, width):
    sources = message.shape[0] // SLOTS
    vmem = pl.BlockSpec(memory_space=pltpu.VMEM)
    shape = lambda *dims: jax.ShapeDtypeStruct(dims, f32)
    return pl.pallas_call(
        bin_kernel,
        out_shape=(
            shape(height, 8, width),
            shape(HALO, 8, width),
            shape(HALO, 8, width),
            shape(height // 64, 8, 128),
            shape(height // 64, 8, 128),
        ),
        in_specs=[vmem],
        out_specs=(vmem,) * 5,
        scratch_shapes=[
            pltpu.VMEM((sources, 128), i32),
            pltpu.SMEM((sources, 128), i32),
            pltpu.SemaphoreType.DMA,
        ],
        compiler_params=pltpu.CompilerParams(vmem_limit_bytes=48 << 20),
        name="bin",
    )(message)


def smooth_row(above, current, below, along_x, along_y):
    total = current.shape[1]
    east = pltpu.roll(current, total - 1, 1)
    west = pltpu.roll(current, 1, 1)
    east_west = east + west - 2.0 * current
    north_south = below + above - 2.0 * current
    return current + along_x * east_west + along_y * north_south


def smooth_kernel(
    flags_ref,
    acc_ref,
    up_ref,
    down_ref,
    west_ref,
    east_ref,
    cx_ref,
    cy_ref,
    gridded_ref,
    coverage_ref,
    ext,
    once,
    twice,
):
    height, _, width = acc_ref.shape
    has_up, has_down = flags_ref[0], flags_ref[1]
    has_west, has_east = flags_ref[2], flags_ref[3]
    lane = iota((8, 128), 1)
    blank = jnp.zeros((8, 128), f32)

    ext[HALO : HALO + height, :, 0:width] = acc_ref[...]
    ext[0:HALO, :, 0:width] = jnp.where(has_up > 0, up_ref[...], 0.0)
    ext[HALO + height :, :, 0:width] = jnp.where(has_down > 0, down_ref[...], 0.0)

    @pl.loop(0, 64)
    def _(j):
        for q in range(4):
            east = pltpu.roll(east_ref[q], 128 - 2 * j, 1)
            west = pltpu.roll(west_ref[q], 126 - 2 * j, 1)
            east = jnp.where((lane < 2) & (has_east > 0), east, 0.0)
            side = jnp.where((lane >= 126) & (has_west > 0), west, east)
            ext[HALO + q * 64 + j, :, width:] = side

    for tile, row, flag in ((4, HALO - 1, has_up), (5, HALO + height, has_down)):
        east = jnp.where((lane < 1) & (has_east > 0), east_ref[tile], 0.0)
        side = jnp.where((lane >= 127) & (has_west > 0), west_ref[tile], east)
        ext[row, :, width:] = jnp.where(flag > 0, side, 0.0)
    ext[0, :, width:] = blank
    ext[HALO + height + 1, :, width:] = blank

    @pl.loop(0, height + 2)
    def _(r):
        once[r] = smooth_row(
            ext[r], ext[r + 1], ext[r + 2], cx_ref[pl.ds(r, 1), :], cy_ref[pl.ds(r, 1), :]
        )

    @pl.loop(0, height)
    def _(r):
        along_x = cx_ref[pl.ds(r + 1, 1), :]
        along_y = cy_ref[pl.ds(r + 1, 1), :]
        fresh = smooth_row(once[r], once[r + 1], once[r + 2], along_x, along_y)
        for half in range(width // 128):
            twice[half, pl.ds(pl.multiple_of(r * 8, 8), 8), :] = fresh[
                :, half * 128 : half * 128 + 128
            ]

    @pl.loop(0, height // 8)
    def _(g):
        rows = pl.ds(pl.multiple_of(g * 8, 8), 8)
        for half in range(width // 128):
            cols = pl.ds(half * 128, 128)
            coverage = twice[half, pl.ds(g * 64 + 6, 8, stride=8), :]
            coverage_ref[rows, cols] = coverage
            scale = 1.0 / jnp.maximum(coverage, FLOOR)
            for c in range(6):
                gridded_ref[c, rows, cols] = twice[half, pl.ds(g * 64 + c, 8, stride=8), :] * scale


def smooth(flags, acc, up, down, west, east, cx, cy):
    height, _, width = acc.shape
    vmem = pl.BlockSpec(memory_space=pltpu.VMEM)
    return pl.pallas_call(
        smooth_kernel,
        out_shape=(
            jax.ShapeDtypeStruct((6, height, width), f32),
            jax.ShapeDtypeStruct((height, width), f32),
        ),
        in_specs=[pl.BlockSpec(memory_space=pltpu.SMEM)] + [vmem] * 7,
        out_specs=(vmem, vmem),
        scratch_shapes=[
            pltpu.VMEM((height + 2 * HALO, 8, width + 128), f32),
            pltpu.VMEM((height + 2, 8, width + 128), f32),
            pltpu.VMEM((width // 128, height * 8, 128), f32),
        ],
        compiler_params=pltpu.CompilerParams(vmem_limit_bytes=48 << 20),
        name="smooth",
    )(flags, acc, up, down, west, east, cx, cy)


def extend(block, up, down, west, east, flags):
    height, width = block.shape
    up = jnp.where(flags[0] > 0, up, 0.0)
    down = jnp.where(flags[1] > 0, down, 0.0)
    west = jnp.where(flags[2] > 0, west, 0.0)
    east = jnp.where(flags[3] > 0, east, 0.0)
    core = jnp.concatenate([up[None], block, down[None]], axis=0)
    middle = jnp.zeros((height, 126), f32)
    side = jnp.concatenate([east[:, None], middle, west[:, None]], axis=1)
    side = jnp.pad(side, ((1, 1), (0, 0)))
    return jnp.concatenate([core, side], axis=1)


def body(swath_bands, clear_weight, owners, tile_row, columns, counts, conduct_x, conduct_y):
    blocks = swath_bands.shape[0]
    height, width = conduct_x.shape
    across, along = lax.axis_size("gx"), lax.axis_size("gy")
    devices = across * along
    gx, gy = lax.axis_index("gx"), lax.axis_index("gy")
    flags = jnp.stack([gy > 0, gy < along - 1, gx > 0, gx < across - 1]).astype(i32)
    message = pack(
        counts,
        owners.reshape(1, blocks),
        tile_row.reshape(1, blocks),
        swath_bands,
        clear_weight,
        columns,
        devices,
    )
    arrived = lax.all_to_all(
        message.reshape(devices, SLOTS, 8, 128),
        ("gx", "gy"),
        split_axis=0,
        concat_axis=0,
        tiled=True,
    ).reshape(devices * SLOTS, 8, 128)

    both = jnp.stack([conduct_x, conduct_y])
    from_up = lax.ppermute(both[:, height - 1, :], "gy", ring(along, 1))
    from_down = lax.ppermute(both[:, 0, :], "gy", ring(along, -1))
    from_west = lax.ppermute(both[:, :, width - 1], "gx", ring(across, 1))
    from_east = lax.ppermute(both[:, :, 0], "gx", ring(across, -1))
    cx, cy = (
        extend(both[i], from_up[i], from_down[i], from_west[i], from_east[i], flags)
        for i in range(2)
    )

    acc, top, bottom, left, right = bin_blocks(arrived, height, width)
    up = lax.ppermute(bottom, "gy", ring(along, 1))
    down = lax.ppermute(top, "gy", ring(along, -1))
    near = jnp.concatenate([left, up[1:2, :, 0:128], down[0:1, :, 0:128]], axis=0)
    far = jnp.concatenate([right, up[1:2, :, width - 128 :], down[0:1, :, width - 128 :]], axis=0)
    west = lax.ppermute(far, "gx", ring(across, 1))
    east = lax.ppermute(near, "gx", ring(across, -1))
    return smooth(flags, acc, up, down, west, east, cx, cy)


def solution(mesh):
    return jax.shard_map(
        body,
        mesh=mesh,
        in_specs=(
            P(("gx", "gy"), None, None),
            P(("gx", "gy"), None),
            P(("gx", "gy"), None),
            P(("gx", "gy")),
            P(("gx", "gy"), None),
            P(("gx", "gy")),
            P("gy", "gx"),
            P("gy", "gx"),
        ),
        out_specs=(P(None, "gy", "gx"), P("gy", "gx")),
        check_vma=False,
    )
```

time: 325 us -> 182 us (0.56)
  the two profiles are of different devices: /device:TPU:10 before, /device:TPU:0 now
where the time goes in v1:
time: 182 us; the launch traced here: 181 us
  Pallas kernels  105 us (58%)
  waiting for transfers between devices  27.9 us (15%)
  starting transfers between devices  24.7 us (14%)
  local copies, waits for them, and re-layouts  12.7 us (7%)
  other arithmetic  6.92 us (4%)
  between operations  4.04 us (2%)
    pallas_call x1, Pallas kernels, bin_blocks(): pl.pallas_call(bin_kernel, out_shape=(shape(height, 8, width), shape(HALO...  51.1 us
    pallas_call x1, Pallas kernels, smooth(): pl.pallas_call(smooth_kernel, out_shape=(jax.ShapeDtypeStruct((6, height,...  48.1 us
    ppermute x1, waiting for transfers between devices, body(): from_west = lax.ppermute(both[:, :, width - 1], 'gx', ring(across, 1))  21.8 us
    all_to_all x1, starting transfers between devices, body(): lax.all_to_all(message.reshape(devices, SLOTS, 8, 128), ('gx', 'gy'), spl...  11 us
    pallas_call x1, Pallas kernels, pack(): pl.pallas_call(pack_kernel, out_shape=jax.ShapeDtypeStruct((devices * SLO...  5.51 us
    ppermute x1, starting transfers between devices, body(): east = lax.ppermute(near, 'gx', ring(across, -1))  5.34 us
    ppermute x1, starting transfers between devices, body(): from_east = lax.ppermute(both[:, :, 0], 'gx', ring(across, -1))  4.27 us
    ppermute x1, waiting for transfers between devices, body(): up = lax.ppermute(bottom, 'gy', ring(along, 1))  3.69 us
  transfers between devices with their start and end apart: 9, of which 4 were waited for; matrix products, arithmetic and copies ran while one was open for 9% of the time, Pallas kernels for 28%

profile of v1, /device:TPU:0, one launch (start us, length us, event | category | flops | bytes accessed | tf_op | source)
XLA Modules:
  0.0 180.9 jit_solution(9977004294934436593)
XLA Ops:
  0.6 0.0 copy-start.2
  0.6 0.0 copy-start.3
  0.7 0.0 copy-start.1
  0.7 0.0 copy-start
  1.4 2.5 %copy.21.swath_ref = bf16[1024,6,128]{2,1,0:T(8,128)(2,1)S(1)} copy(bf16[1024,6,128]{2,0,1:T(8,128)(2,1)} %param.8) | data formatting | bytes 3145728 | tf_op args[0]
  3.9 0.0 copy-done.2
  3.9 0.0 copy-done.3
  3.9 0.0 copy-done.1
  3.9 0.0 copy-done
  3.9 5.5 %pack.1 = bf16[1664,8,128]{2,1,0:T(8,128)(2,1)} custom-call(s32[1]{0:T(128)S(6)} %copy.32.count_ref, s32[1,1024]{1,0:T(1,128)S(1)} %bitcast.29, s32[1,1024]{1,0:T(1,128)S(1)} %bitcast.30, bf16[1024,6,128]{2,1,0:T(8,128)(2,1)S(1)} %copy.21.swath_ref, bf16[1024,128]{1,0:T(8,128)(2,1)S(1)} %copy-done.1, s32[1024,128]{1,0:T(8,128)S(1)} %copy-done), custom_call_target="tpu_custom_call" | custom-call | tf_op jit(solution)/shard_map/pack/pallas_call | solution.py:91
  9.4 11.0 %all-to-all-start = ((bf16[128,13,8,128]{3,2,1,0:T(8,128)(2,1)}), bf16[128,13,8,128]{3,2,1,0:T(8,128)(2,1)S(1)}, u32[]{:S(2)}, u32[]{:S(2)}) async-start(bf16[128,13,8,128]{3,2,1,0:T(8,128)(2,1)} %bitcast.31), calls=%async_computation | async-start | bytes 6815744 | tf_op jit(solution)/shard_map/all_to_all | solution.py:333
  20.4 1.8 copy.31
  22.2 1.8 copy.30
  24.0 0.7 fusion.4
  24.7 1.1 collective-permute-start.7
  25.9 4.3 %collective-permute-start.6 = (f32[2,256]{1,0:T(2,128)S(1)}, f32[2,256]{1,0:T(2,128)S(1)}, u32[]{:S(2)}, u32[]{:S(2)}) collective-permute-start(f32[2,256]{1,0:T(2,128)S(1)} %get-tuple-element.14), channel_id=1, source_target_pairs={{0,120},{8,0},{16,8},{24,16},{32,24},{40,32},{48,40},{56,48},{64,5... | collective-permute-start | bytes 6152 | tf_op jit(solution)/shard_map/ppermute | solution.py:345
  30.1 2.6 %fusion = (f32[2,1,256]{1,0,2:T(2,128)}, f32[2,1,256]{1,0,2:T(2,128)}) fusion(f32[1,256,256]{1,0,2:T(1,128)} %copy.30, f32[1,256,256]{1,0,2:T(1,128)} %copy.31), kind=kLoop, calls=%fused_computation.9 | loop fusion | flops 1024 | bytes 528384 | tf_op jit(solution)/shard_map/stack | solution.py:341
  32.8 1.1 copy.25
  33.8 2.1 %collective-permute-start.5 = (f32[2,256]{1,0:T(2,128)S(1)}, f32[2,256]{1,0:T(2,128)}, u32[]{:S(2)}, u32[]{:S(2)}) collective-permute-start(f32[2,256]{1,0:T(2,128)S(1)} %bitcast.35), channel_id=1, source_target_pairs={{0,7},{1,0},{2,1},{3,2},{4,3},{5,4},{6,5},{7,6},{8,15},{9,8},{10,9... | collective-permute-start | bytes 6152 | tf_op jit(solution)/shard_map/ppermute | solution.py:343
  35.9 1.1 copy.24
  37.0 0.0 collective-permute-start.4
  37.0 0.1 add_convert_fusion.flags_ref
  37.1 0.7 fusion.11
  40.3 0.6 pad.21.clone
  40.9 21.8 %collective-permute-done.7 = f32[2,256]{1,0:T(2,128)S(1)} collective-permute-done((f32[2,256]{1,0:T(2,128)S(1)}, f32[2,256]{1,0:T(2,128)S(1)}, u32[]{:S(2)}, u32[]{:S(2)}) %collective-permute-start.7) | collective-permute-done | bytes 2080 | tf_op jit(solution)/shard_map/ppermute | solution.py:344
  62.7 0.8 copy.29
  63.5 0.0 collective-permute-done.6
  63.5 0.8 copy.28
  64.3 0.8 copy.27
  65.1 0.8 copy.26
  65.9 1.9 %pad_maximum_fusion.1 = (f32[256,128]{1,0:T(8,128)S(1)}, f32[256,128]{1,0:T(8,128)}) fusion(f32[256,1]{1,0:T(8,128)} %copy.29, f32[256,1]{1,0:T(8,128)} %copy.28, f32[128]{0:T(128)} %pad.21.clone, f32[256,1]{1,0:T(8,128)} %copy.27, f32[256,1]{1,0:T(8,128)} %copy.26), kind=kLoop, calls=%fused_computation.12 | loop fusion | flops 131072 | bytes 266752 | tf_op jit(solution)/shard_map/concatenate | solution.py:312
  67.8 0.0 collective-permute-done.5
  67.8 0.7 broadcast_select_fusion.4
  68.5 0.0 all-to-all-done
  68.5 0.0 copy-start.4
  68.5 0.0 copy-start.5
  68.5 0.0 copy-start.6
  68.5 51.1 %bin.1 = (f32[256,8,256]{2,1,0:T(8,128)S(1)}, f32[2,8,256]{2,1,0:T(8,128)S(1)}, f32[2,8,256]{2,1,0:T(8,128)S(1)}, f32[4,8,128]{2,1,0:T(8,128)S(1)}, f32[4,8,128]{2,1,0:T(8,128)S(1)}) custom-call(bf16[1664,8,128]{2,1,0:T(8,128)(2,1)S(1)} %bitcast.28), custom_call_target="tpu_custom_call" | custom-call | tf_op jit(solution)/shard_map/bin/pallas_call | solution.py:184
  119.6 0.9 collective-permute-start.1
  120.5 0.0 collective-permute-done.4
  120.5 0.8 broadcast_select_fusion.6
  121.2 0.0 collective-permute-start
  121.2 0.7 collective-permute-done.1.down_ref
  121.9 3.7 %collective-permute-done.up_ref = f32[2,8,256]{2,1,0:T(8,128)S(1)} collective-permute-done((f32[2,8,256]{2,1,0:T(8,128)S(1)}, f32[2,8,256]{2,1,0:T(8,128)S(1)}, u32[]{:S(2)}, u32[]{:S(2)}) %collective-permute-start) | collective-permute-done | bytes 16416 | tf_op jit(solution)/shard_map/ppermute | solution.py:352
  125.6 0.0 collective-permute-start.2
  125.6 5.3 %collective-permute-start.3 = (f32[6,8,128]{2,1,0:T(8,128)S(1)}, f32[6,8,128]{2,1,0:T(8,128)S(1)}, u32[]{:S(2)}, u32[]{:S(2)}) collective-permute-start(f32[6,8,128]{2,1,0:T(8,128)S(1)} %pad_maximum_fusion.3), channel_id=1, source_target_pairs={{0,120},{8,0},{16,8},{24,16},{32,24},{40,32},{48,40},{56,48},{64,5... | collective-permute-start | bytes 73736 | tf_op jit(solution)/shard_map/ppermute | solution.py:357
  131.0 0.0 copy-done.4
  131.0 0.0 copy-done.5
  131.0 0.0 copy-done.6
  131.0 0.1 select_maximum_fusion
  131.1 1.7 collective-permute-done.2.west_ref
  132.8 0.0 collective-permute-done.3.east_ref
  132.8 48.1 %smooth.1 = (f32[6,256,256]{2,1,0:T(8,128)}, f32[256,256]{1,0:T(8,128)}) custom-call(s32[4]{0:T(128)S(1)} %add_convert_fusion.flags_ref, f32[256,8,256]{2,1,0:T(8,128)S(1)} %get-tuple-element.7.acc_ref, f32[2,8,256]{2,1,0:T(8,128)S(1)} %collective-permute-done.up_ref, f32[2,8,256]{2,1,0:T(8,128)S(1)} %collective-permute-done.1.down_ref, ...), custom_call_target="tpu_custom_call" | custom-call | tf_op jit(solution)/shard_map/smooth/pallas_call | solution.py:286
  (7 shorter events, 0.0 us)
Async XLA Ops:
  0.6 3.3 %copy-start.2 = (s32[1024,1]{0,1:T(1,128)S(1)}, s32[1024,1]{0,1:T(1,128)}, u32[]{:S(2)}) copy-start(s32[1024,1]{0,1:T(1,128)} %param.10) | copy-start | bytes 12292
  0.6 3.3 %copy-start.3 = (s32[1024]{0:T(1024)S(1)}, s32[1024]{0:T(1024)}, u32[]{:S(2)}) copy-start(s32[1024]{0:T(1024)} %param.11) | copy-start | bytes 12292
  0.7 3.3 %copy-start.1 = (bf16[1024,128]{1,0:T(8,128)(2,1)S(1)}, bf16[1024,128]{1,0:T(8,128)(2,1)}, u32[]{:S(2)}) copy-start(bf16[1024,128]{1,0:T(8,128)(2,1)} %weight_ref.1) | copy-start | bytes 786436
  0.7 3.3 %copy-start = (s32[1024,128]{1,0:T(8,128)S(1)}, s32[1024,128]{1,0:T(8,128)}, u32[]{:S(2)}) copy-start(s32[1024,128]{1,0:T(8,128)} %cols_ref.1) | copy-start | bytes 1572868
  9.4 59.1 %all-to-all-start = ((bf16[128,13,8,128]{3,2,1,0:T(8,128)(2,1)}), bf16[128,13,8,128]{3,2,1,0:T(8,128)(2,1)S(1)}, u32[]{:S(2)}, u32[]{:S(2)}) async-start(bf16[128,13,8,128]{3,2,1,0:T(8,128)(2,1)} %bitcast.31), calls=%async_computation | async-start | bytes 6815744 | tf_op jit(solution)/shard_map/all_to_all | solution.py:333
  24.7 37.9 %collective-permute-start.7 = (f32[2,256]{1,0:T(2,128)S(1)}, f32[2,256]{1,0:T(2,128)S(1)}, u32[]{:S(2)}, u32[]{:S(2)}) collective-permute-start(f32[2,256]{1,0:T(2,128)S(1)} %get-tuple-element.15), channel_id=1, source_target_pairs={{0,8},{8,16},{16,24},{24,32},{32,40},{40,48},{48,56},{56,64},{64,7... | collective-permute-start | bytes 6152 | tf_op jit(solution)/shard_map/ppermute | solution.py:344
  25.9 37.6 %collective-permute-start.6 = (f32[2,256]{1,0:T(2,128)S(1)}, f32[2,256]{1,0:T(2,128)S(1)}, u32[]{:S(2)}, u32[]{:S(2)}) collective-permute-start(f32[2,256]{1,0:T(2,128)S(1)} %get-tuple-element.14), channel_id=1, source_target_pairs={{0,120},{8,0},{16,8},{24,16},{32,24},{40,32},{48,40},{56,48},{64,5... | collective-permute-start | bytes 6152 | tf_op jit(solution)/shard_map/ppermute | solution.py:345
  33.8 33.9 %collective-permute-start.5 = (f32[2,256]{1,0:T(2,128)S(1)}, f32[2,256]{1,0:T(2,128)}, u32[]{:S(2)}, u32[]{:S(2)}) collective-permute-start(f32[2,256]{1,0:T(2,128)S(1)} %bitcast.35), channel_id=1, source_target_pairs={{0,7},{1,0},{2,1},{3,2},{4,3},{5,4},{6,5},{7,6},{8,15},{9,8},{10,9... | collective-permute-start | bytes 6152 | tf_op jit(solution)/shard_map/ppermute | solution.py:343
  37.0 83.5 %collective-permute-start.4 = (f32[2,256]{1,0:T(2,128)S(1)}, f32[2,256]{1,0:T(2,128)}, u32[]{:S(2)}, u32[]{:S(2)}) collective-permute-start(f32[2,256]{1,0:T(2,128)S(1)} %bitcast.34), channel_id=1, source_target_pairs={{0,1},{1,2},{2,3},{3,4},{4,5},{5,6},{6,7},{7,0},{8,9},{9,10},{10,1... | collective-permute-start | bytes 6152 | tf_op jit(solution)/shard_map/ppermute | solution.py:342
  68.5 62.5 %copy-start.4 = (f32[256,256]{1,0:T(8,128)S(1)}, f32[256,256]{1,0:T(8,128)}, u32[]{:S(2)}) copy-start(f32[256,256]{1,0:T(8,128)} %param.15) | copy-start | bytes 786436
  68.5 62.5 %copy-start.5 = (f32[256,256]{1,0:T(8,128)S(1)}, f32[256,256]{1,0:T(8,128)}, u32[]{:S(2)}) copy-start(f32[256,256]{1,0:T(8,128)} %param.14) | copy-start | bytes 786436
  68.5 62.5 %copy-start.6 = (f32[256,128]{1,0:T(8,128)S(1)}, f32[256,128]{1,0:T(8,128)}, u32[]{:S(2)}) copy-start(f32[256,128]{1,0:T(8,128)} %get-tuple-element.29) | copy-start | bytes 393220
  119.6 2.3 %collective-permute-start.1 = (f32[2,8,256]{2,1,0:T(8,128)S(1)}, f32[2,8,256]{2,1,0:T(8,128)S(1)}, u32[]{:S(2)}, u32[]{:S(2)}) collective-permute-start(f32[2,8,256]{2,1,0:T(8,128)S(1)} %get-tuple-element.9), channel_id=1, source_target_pairs={{0,7},{1,0},{2,1},{3,2},{4,3},{5,4},{6,5},{7,6},{8,15},{9,8},{10,9... | collective-permute-start | bytes 49160 | tf_op jit(solution)/shard_map/ppermute | solution.py:353
  121.2 4.4 %collective-permute-start = (f32[2,8,256]{2,1,0:T(8,128)S(1)}, f32[2,8,256]{2,1,0:T(8,128)S(1)}, u32[]{:S(2)}, u32[]{:S(2)}) collective-permute-start(f32[2,8,256]{2,1,0:T(8,128)S(1)} %get-tuple-element.8), channel_id=1, source_target_pairs={{0,1},{1,2},{2,3},{3,4},{4,5},{5,6},{6,7},{7,0},{8,9},{9,10},{10,1... | collective-permute-start | bytes 49160 | tf_op jit(solution)/shard_map/ppermute | solution.py:352
  125.6 7.1 %collective-permute-start.2 = (f32[6,8,128]{2,1,0:T(8,128)S(1)}, f32[6,8,128]{2,1,0:T(8,128)S(1)}, u32[]{:S(2)}, u32[]{:S(2)}) collective-permute-start(f32[6,8,128]{2,1,0:T(8,128)S(1)} %pad_maximum_fusion.2), channel_id=1, source_target_pairs={{0,8},{8,16},{16,24},{24,32},{32,40},{40,48},{48,56},{56,64},{64,7... | collective-permute-start | bytes 73736 | tf_op jit(solution)/shard_map/ppermute | solution.py:356
  125.6 7.1 %collective-permute-start.3 = (f32[6,8,128]{2,1,0:T(8,128)S(1)}, f32[6,8,128]{2,1,0:T(8,128)S(1)}, u32[]{:S(2)}, u32[]{:S(2)}) collective-permute-start(f32[6,8,128]{2,1,0:T(8,128)S(1)} %pad_maximum_fusion.3), channel_id=1, source_target_pairs={{0,120},{8,0},{16,8},{24,16},{32,24},{40,32},{48,40},{56,48},{64,5... | collective-permute-start | bytes 73736 | tf_op jit(solution)/shard_map/ppermute | solution.py:357

commit v2 on v1

v2 whole, which is shorter than its diff:
```python
import functools

import jax
import jax.numpy as jnp
from jax import lax
from jax.experimental import pallas as pl
from jax.experimental.pallas import tpu as pltpu
from jax.sharding import PartitionSpec as P

CAPACITY = 12
SLOTS = CAPACITY + 1
COUNT_LANE = 16
GROUP = 64
ROWS = 16
FLOOR = 0.15
HALO = 2

f32 = jnp.float32
bf16 = jnp.bfloat16
i32 = jnp.int32


def iota(shape, dim):
    return lax.broadcasted_iota(i32, shape, dim)


def ring(count, step):
    return [(i, (i + step) % count) for i in range(count)]


def pack_kernel(
    count_ref,
    owner_ref,
    row_ref,
    swath_ref,
    weight_ref,
    cols_ref,
    out_ref,
    done_ref,
    owner_v,
    row_v,
    swath_v,
    weight_v,
    cols_v,
    rows_f,
    codes_f,
    slot_v,
    slot_s,
    sem,
    load_sems,
):
    bands, blocks, _ = swath_ref.shape
    loads = [
        pltpu.make_async_copy(source, target, load_sems.at[i])
        for i, (source, target) in enumerate(
            (
                (owner_ref, owner_v),
                (row_ref, row_v),
                (weight_ref, weight_v),
                (cols_ref, cols_v),
                (swath_ref, swath_v),
            )
        )
    ]
    for load in loads:
        load.start()
    done_ref[...] = jnp.zeros((8, 128), f32)
    devices = out_ref.shape[0] // SLOTS
    live_count = count_ref[0]
    loads[0].wait()
    owner = owner_v[...]
    live = iota((1, blocks), 1) < live_count
    owner = jnp.where(live, owner, -1)
    named = (iota((devices, blocks), 0) == owner).astype(f32)
    named16 = named.astype(bf16)
    earlier = (iota((blocks, blocks), 0) < iota((blocks, blocks), 1)).astype(f32).astype(bf16)
    before = jnp.dot(named16, earlier, preferred_element_type=f32)
    rank = jnp.sum(named * before, axis=0, keepdims=True).astype(i32)
    slot_v[...] = jnp.where(live, owner * SLOTS + rank, CAPACITY)
    copy = pltpu.make_async_copy(slot_v, slot_s, sem)
    copy.start()
    entry = iota((128, blocks), 0)
    loads[1].wait()
    place = jnp.where(entry == rank, (row_v[...] + 1).astype(f32), 0.0)
    place = jnp.where(entry == COUNT_LANE, 1.0, place).astype(bf16)
    codes_f[...] = lax.dot_general(
        named16, place, (((1,), (1,)), ((), ())), preferred_element_type=f32
    )

    @pl.loop(0, devices)
    def _(t):
        out_ref[pl.ds(t * SLOTS, SLOTS)] = jnp.zeros((SLOTS, 8, 128), bf16)

    for load in loads[2:]:
        load.wait()

    @pl.loop(0, blocks // 16, unroll=4)
    def _(g):
        near = pl.ds(pl.multiple_of(g * 16, 16), 16)
        weight = weight_v[near, :].astype(f32)
        for c in range(bands):
            rows_f[pl.ds(g * 128 + c, 16, stride=8), :] = swath_v[c, near, :].astype(f32) * weight
        rows_f[pl.ds(g * 128 + bands, 16, stride=8), :] = weight
        rows_f[pl.ds(g * 128 + bands + 1, 16, stride=8), :] = cols_v[near, :].astype(f32)

    copy.wait()

    @pl.loop(0, (live_count + 15) // 16)
    def _(group):
        for i in range(16):
            b = group * 16 + i
            out_ref[slot_s[0, b]] = rows_f[pl.ds(pl.multiple_of(b * 8, 8), 8), :].astype(bf16)

    @pl.loop(0, devices, unroll=4)
    def _(t):
        code = codes_f[pl.ds(t, 1), :]
        out_ref[t * SLOTS + CAPACITY] = jnp.broadcast_to(code, (8, 128)).astype(bf16)


def pack(counts, owners, tile_row, swath, weight, columns, devices):
    blocks = weight.shape[0]
    vmem = pl.BlockSpec(memory_space=pltpu.VMEM)
    return pl.pallas_call(
        pack_kernel,
        out_shape=(
            jax.ShapeDtypeStruct((devices * SLOTS, 8, 128), bf16),
            jax.ShapeDtypeStruct((8, 128), f32),
        ),
        in_specs=[pl.BlockSpec(memory_space=pltpu.SMEM)]
        + [pl.BlockSpec(memory_space=pltpu.HBM)] * 5,
        out_specs=(vmem, vmem),
        scratch_shapes=[
            pltpu.VMEM((1, blocks), i32),
            pltpu.VMEM((1, blocks), i32),
            pltpu.VMEM(swath.shape, bf16),
            pltpu.VMEM(weight.shape, bf16),
            pltpu.VMEM(columns.shape, i32),
            pltpu.VMEM((blocks * 8, 128), f32),
            pltpu.VMEM((devices, 128), f32),
            pltpu.VMEM((1, blocks), i32),
            pltpu.SMEM((1, blocks), i32),
            pltpu.SemaphoreType.DMA,
            pltpu.SemaphoreType.DMA((5,)),
        ],
        compiler_params=pltpu.CompilerParams(vmem_limit_bytes=60 << 20),
        name="pack",
    )(counts, owners, tile_row, swath, weight, columns)


def bin_kernel(
    msg_ref,
    after_ref,
    acc_ref,
    top_ref,
    bottom_ref,
    left_ref,
    right_ref,
    codes_v,
    codes_s,
    pairs_s,
    sem,
):
    sources = msg_ref.shape[0] // SLOTS
    height, width = acc_ref.shape[0] - 1, acc_ref.shape[2]

    @pl.loop(0, sources // 8)
    def _(g):
        for i in range(8):
            s = g * 8 + i
            tile = msg_ref[s * SLOTS + CAPACITY].astype(f32)
            codes_v[pl.ds(s, 1), :] = tile[0:1, :].astype(i32)

    copy = pltpu.make_async_copy(codes_v, codes_s, sem)
    copy.start()

    @pl.loop(0, height // 16)
    def _(g):
        acc_ref[pl.ds(g * 16, 16)] = jnp.zeros((16, 8, width), f32)

    acc_ref[height] = jnp.zeros((8, width), f32)
    copy.wait()

    def note_source(s, total):
        for p in range(CAPACITY // 2):
            pairs_s[total + p] = s * 128 + 2 * p
        return total + (codes_s[s, COUNT_LANE] + 1) // 2

    total = lax.fori_loop(0, sources, note_source, 0)

    @pl.loop(0, GROUP // 8)
    def _(g):
        for i in range(8):
            pairs_s[total + g * 8 + i] = CAPACITY

    low_ids = iota((64, 128), 0).astype(f32)
    quarter_ids = (iota((32, 128), 0) // 8).astype(f32)
    empty = jnp.zeros((32, 128), bf16)

    @pl.loop(0, (total + GROUP - 1) // GROUP)
    def _(group):
        for j in range(GROUP):
            pair = pairs_s[group * GROUP + j]
            source, first = pair // 128, pair % 128
            slot = source * SLOTS + first
            values, hits = [], []
            for i in range(2):
                block = msg_ref[slot + i].astype(f32)
                col = block[7:8, :]
                quarter = jnp.where(
                    col >= 128.0,
                    jnp.where(col >= 192.0, 3.0, 2.0),
                    jnp.where(col >= 64.0, 1.0, 0.0),
                )
                low = col - 64.0 * quarter
                block4 = jnp.concatenate([block] * 4, axis=0)
                values.append(jnp.where(quarter_ids == quarter, block4, 0.0).astype(bf16))
                hits.append(jnp.where(low_ids == low, 1.0, 0.0).astype(bf16))
            values = jnp.concatenate(
                [
                    jnp.concatenate([values[0], empty], axis=1),
                    jnp.concatenate([empty, values[1]], axis=1),
                ],
                axis=0,
            )
            sums = lax.dot_general(
                values,
                jnp.concatenate(hits, axis=1),
                (((1,), (1,)), ((), ())),
                preferred_element_type=f32,
            )
            for i in range(2):
                code = codes_s[source, first + i]
                row = jnp.where(code > 0, code - 1, height)
                for h in range(2):
                    o = 32 * i + 16 * h
                    acc_ref[row, :, 128 * h : 128 * h + 128] += jnp.concatenate(
                        [sums[o : o + 8], sums[o + 8 : o + 16]], axis=1
                    )

    top_ref[...] = acc_ref[0:HALO]
    bottom_ref[...] = acc_ref[height - HALO : height]
    lane = iota((8, 128), 1)
    blank = jnp.zeros((8, 128), f32)

    def edges(j, carry):
        here = lane // 2 == j
        result = []
        for q in range(4):
            near = pltpu.roll(acc_ref[q * 64 + j, :, 0:128], 2 * j, 1)
            result.append(jnp.where(here, near, carry[2 * q]))
            far = pltpu.roll(acc_ref[q * 64 + j, :, width - 128 : width], 2 * j + 2, 1)
            result.append(jnp.where(here, far, carry[2 * q + 1]))
        return tuple(result)

    strips = lax.fori_loop(0, 64, edges, (blank,) * 8, unroll=8)
    for q in range(4):
        left_ref[q] = strips[2 * q]
        right_ref[q] = strips[2 * q + 1]


def bin_blocks(message, after, height, width):
    sources = message.shape[0] // SLOTS
    vmem = pl.BlockSpec(memory_space=pltpu.VMEM)
    shape = lambda *dims: jax.ShapeDtypeStruct(dims, f32)
    return pl.pallas_call(
        bin_kernel,
        out_shape=(
            shape(height + 1, 8, width),
            shape(HALO, 8, width),
            shape(HALO, 8, width),
            shape(height // 64, 8, 128),
            shape(height // 64, 8, 128),
        ),
        in_specs=[vmem, pl.BlockSpec(memory_space=pl.ANY)],
        out_specs=(vmem,) * 5,
        scratch_shapes=[
            pltpu.VMEM((sources, 128), i32),
            pltpu.SMEM((sources, 128), i32),
            pltpu.SMEM((sources * CAPACITY // 2 + GROUP + 8,), i32),
            pltpu.SemaphoreType.DMA,
        ],
        compiler_params=pltpu.CompilerParams(vmem_limit_bytes=48 << 20),
        name="bin",
    )(message, after)


def smooth_row(above, current, below, along_x, along_y):
    total = current.shape[1]
    east = pltpu.roll(current, total - 1, 1)
    west = pltpu.roll(current, 1, 1)
    east_west = east + west - 2.0 * current
    north_south = below + above - 2.0 * current
    return current + along_x * east_west + along_y * north_south


def smooth_kernel(
    flags_ref,
    acc_ref,
    up_ref,
    down_ref,
    west_ref,
    east_ref,
    cx_ref,
    cy_ref,
    gridded_ref,
    coverage_ref,
    ext,
    once,
    twice,
):
    height, width = acc_ref.shape[0] - 1, acc_ref.shape[2]
    has_up, has_down = flags_ref[0], flags_ref[1]
    has_west, has_east = flags_ref[2], flags_ref[3]
    lane = iota((8, 128), 1)
    blank = jnp.zeros((8, 128), f32)

    ext[HALO : HALO + height, :, 0:width] = acc_ref[0:height]
    ext[0:HALO, :, 0:width] = jnp.where(has_up > 0, up_ref[...], 0.0)
    ext[HALO + height :, :, 0:width] = jnp.where(has_down > 0, down_ref[...], 0.0)

    @pl.loop(0, 64, unroll=16)
    def _(j):
        for q in range(4):
            east = pltpu.roll(east_ref[q], 128 - 2 * j, 1)
            west = pltpu.roll(west_ref[q], 126 - 2 * j, 1)
            east = jnp.where((lane < 2) & (has_east > 0), east, 0.0)
            side = jnp.where((lane >= 126) & (has_west > 0), west, east)
            ext[HALO + q * 64 + j, :, width:] = side

    for tile, row, flag in ((4, HALO - 1, has_up), (5, HALO + height, has_down)):
        east = jnp.where((lane < 1) & (has_east > 0), east_ref[tile], 0.0)
        side = jnp.where((lane >= 127) & (has_west > 0), west_ref[tile], east)
        ext[row, :, width:] = jnp.where(flag > 0, side, 0.0)
    ext[0, :, width:] = blank
    ext[HALO + height + 1, :, width:] = blank

    def pass_rows(source, start, count, shift):
        rows = [source[start + i] for i in range(count + 2)]
        for i in range(count):
            along_x = cx_ref[pl.ds(start + i + shift, 1), :]
            along_y = cy_ref[pl.ds(start + i + shift, 1), :]
            yield i, smooth_row(rows[i], rows[i + 1], rows[i + 2], along_x, along_y)

    for r in (0, height + 1):
        for _, fresh in pass_rows(ext, r, 1, 0):
            once[r] = fresh

    @pl.loop(0, height // ROWS)
    def _(g):
        start = g * ROWS + 1
        for i, fresh in pass_rows(ext, start, ROWS, 0):
            once[start + i] = fresh

    @pl.loop(0, height // ROWS)
    def _(g):
        start = g * ROWS
        for i, fresh in pass_rows(once, start, ROWS, 1):
            for half in range(width // 128):
                twice[half, pl.ds(pl.multiple_of((start + i) * 8, 8), 8), :] = fresh[
                    :, half * 128 : half * 128 + 128
                ]

    @pl.loop(0, height // 8, unroll=2)
    def _(g):
        rows = pl.ds(pl.multiple_of(g * 8, 8), 8)
        for half in range(width // 128):
            cols = pl.ds(half * 128, 128)
            coverage = twice[half, pl.ds(g * 64 + 6, 8, stride=8), :]
            coverage_ref[rows, cols] = coverage
            scale = 1.0 / jnp.maximum(coverage, FLOOR)
            for c in range(6):
                gridded_ref[c, rows, cols] = twice[half, pl.ds(g * 64 + c, 8, stride=8), :] * scale


def smooth(flags, acc, up, down, west, east, cx, cy):
    height, width = acc.shape[0] - 1, acc.shape[2]
    vmem = pl.BlockSpec(memory_space=pltpu.VMEM)
    return pl.pallas_call(
        smooth_kernel,
        out_shape=(
            jax.ShapeDtypeStruct((6, height, width), f32),
            jax.ShapeDtypeStruct((height, width), f32),
        ),
        in_specs=[pl.BlockSpec(memory_space=pltpu.SMEM)] + [vmem] * 7,
        out_specs=(vmem, vmem),
        scratch_shapes=[
            pltpu.VMEM((height + 2 * HALO, 8, width + 128), f32),
            pltpu.VMEM((height + 2, 8, width + 128), f32),
            pltpu.VMEM((width // 128, height * 8, 128), f32),
        ],
        compiler_params=pltpu.CompilerParams(vmem_limit_bytes=48 << 20),
        name="smooth",
    )(flags, acc, up, down, west, east, cx, cy)


def edge_kernel(after_ref, cx_ref, cy_ref, top_ref, bottom_ref, left_ref, right_ref):
    height, width = cx_ref.shape
    for i, block in enumerate((cx_ref, cy_ref)):
        top_ref[i : i + 1, :] = block[0:1, :]
        bottom_ref[i : i + 1, :] = block[height - 1 : height, :]
        left_ref[i : i + 1, :] = block[:, 0:128].T[0:1, :]
        right_ref[i : i + 1, :] = block[:, width - 128 : width].T[127:128, :]


def coefficient_edges(after, cx, cy):
    height, width = cx.shape
    vmem = pl.BlockSpec(memory_space=pltpu.VMEM)
    row = jax.ShapeDtypeStruct((2, width), f32)
    column = jax.ShapeDtypeStruct((2, height), f32)
    return pl.pallas_call(
        edge_kernel,
        out_shape=(row, row, column, column),
        in_specs=[vmem] * 3,
        out_specs=(vmem,) * 4,
        name="coefficient_edges",
    )(after, cx, cy)


def extend_kernel(
    flags_ref, cx_ref, cy_ref, up_ref, down_ref, west_ref, east_ref, ext_x, ext_y, done_ref
):
    done_ref[...] = jnp.zeros((8, 128), f32)
    height, width = cx_ref.shape
    lane = iota((height, 128), 1)
    for i, (block, ext) in enumerate(((cx_ref, ext_x), (cy_ref, ext_y))):
        up = jnp.where(flags_ref[0] > 0, up_ref[i : i + 1, :], 0.0)
        down = jnp.where(flags_ref[1] > 0, down_ref[i : i + 1, :], 0.0)
        west = jnp.where(flags_ref[2] > 0, west_ref[i : i + 1, :], 0.0)
        east = jnp.where(flags_ref[3] > 0, east_ref[i : i + 1, :], 0.0)
        ext[0:1, 0:width] = up
        ext[1 : height + 1, 0:width] = block[...]
        ext[height + 1 : height + 2, 0:width] = down
        west = jnp.broadcast_to(west, (128, height)).T
        east = jnp.broadcast_to(east, (128, height)).T
        side = jnp.where(lane == 0, east, jnp.where(lane == 127, west, 0.0))
        ext[0:1, width:] = jnp.zeros((1, 128), f32)
        ext[1 : height + 1, width:] = side
        ext[height + 1 : height + 2, width:] = jnp.zeros((1, 128), f32)


def extend(flags, cx, cy, up, down, west, east):
    height, width = cx.shape
    vmem = pl.BlockSpec(memory_space=pltpu.VMEM)
    wide = jax.ShapeDtypeStruct((height + 2, width + 128), f32)
    return pl.pallas_call(
        extend_kernel,
        out_shape=(wide, wide, jax.ShapeDtypeStruct((8, 128), f32)),
        in_specs=[pl.BlockSpec(memory_space=pltpu.SMEM)] + [vmem] * 6,
        out_specs=(vmem,) * 3,
        name="extend",
    )(flags, cx, cy, up, down, west, east)


def body(swath_bands, clear_weight, owners, tile_row, columns, counts, conduct_x, conduct_y):
    blocks = swath_bands.shape[0]
    height, width = conduct_x.shape
    across, along = lax.axis_size("gx"), lax.axis_size("gy")
    devices = across * along
    gx, gy = lax.axis_index("gx"), lax.axis_index("gy")
    flags = jnp.stack([gy > 0, gy < along - 1, gx > 0, gx < across - 1]).astype(i32)
    message, packed = pack(
        counts,
        owners.reshape(1, blocks),
        tile_row.reshape(1, blocks),
        jnp.transpose(swath_bands, (1, 0, 2)),
        clear_weight,
        columns,
        devices,
    )
    arrived = lax.all_to_all(
        message.reshape(devices, SLOTS, 8, 128),
        ("gx", "gy"),
        split_axis=0,
        concat_axis=0,
        tiled=True,
    ).reshape(devices * SLOTS, 8, 128)

    first_rows, last_rows, first_cols, last_cols = coefficient_edges(packed, conduct_x, conduct_y)
    cx, cy, extended = extend(
        flags,
        conduct_x,
        conduct_y,
        lax.ppermute(last_rows, "gy", ring(along, 1)),
        lax.ppermute(first_rows, "gy", ring(along, -1)),
        lax.ppermute(last_cols, "gx", ring(across, 1)),
        lax.ppermute(first_cols, "gx", ring(across, -1)),
    )

    acc, top, bottom, left, right = bin_blocks(arrived, extended, height, width)
    up = lax.ppermute(bottom, "gy", ring(along, 1))
    down = lax.ppermute(top, "gy", ring(along, -1))
    near = jnp.concatenate([left, up[1:2, :, 0:128], down[0:1, :, 0:128]], axis=0)
    far = jnp.concatenate([right, up[1:2, :, width - 128 :], down[0:1, :, width - 128 :]], axis=0)
    west = lax.ppermute(far, "gx", ring(across, 1))
    east = lax.ppermute(near, "gx", ring(across, -1))
    return smooth(flags, acc, up, down, west, east, cx, cy)


def solution(mesh):
    return jax.shard_map(
        body,
        mesh=mesh,
        in_specs=(
            P(("gx", "gy"), None, None),
            P(("gx", "gy"), None),
            P(("gx", "gy"), None),
            P(("gx", "gy")),
            P(("gx", "gy"), None),
            P(("gx", "gy")),
            P("gy", "gx"),
            P("gy", "gx"),
        ),
        out_specs=(P(None, "gy", "gx"), P("gy", "gx")),
        check_vma=False,
    )
```

time: 182 us -> 102 us (0.56)
  Pallas kernels: 105 us -> 29.4 us
  local copies, waits for them, and re-layouts: 12.7 us -> 1.93 us
  waiting for transfers between devices: 27.9 us -> 37.6 us
  other arithmetic: 6.92 us -> 0.66 us
  starting transfers between devices: 24.7 us -> 29.3 us
  between operations: 4.04 us -> 1.37 us
    pallas_call x1, Pallas kernels: 48.1 us -> 8.85 us  [smooth(): pl.pallas_call(smooth_kernel, out_shape=(jax.ShapeDtypeStruct((6, height,...]
    pallas_call x2 -> x4, Pallas kernels: 56.6 us -> 20.5 us  [the longest x1 10.8 us: bin_blocks(): pl.pallas_call(bin_kernel, out_shape=(shape(height + 1, 8, width), shape(...]
    ppermute x4, waiting for transfers between devices: 21.8 us -> 31.4 us  [the longest x1 25.1 us: body(): lax.ppermute(last_rows, 'gy', ring(along, 1))]
    another operation x3 -> x0, local copies, waits for them, and re-layouts: 3.58 us -> none  [the longest x2 3.57 us: body(): both = jnp.stack([conduct_x, conduct_y])]
    ppermute x1, starting transfers between devices: 0.86 us -> 4.19 us  [body(): down = lax.ppermute(top, 'gy', ring(along, -1))]
    select_n x4 -> x0, local copies, waits for them, and re-layouts: 3.21 us -> none  [the longest x2 1.62 us: extend(): west = jnp.where(flags[2] > 0, west, 0.0)]
    slice x3 -> x0, local copies, waits for them, and re-layouts: 2.77 us -> none  [the longest x1 1.06 us: body(): from_down = lax.ppermute(both[:, 0, :], 'gy', ring(along, -1))]
    another operation x1 -> x0, other arithmetic: 2.65 us -> none  [body(): both = jnp.stack([conduct_x, conduct_y])]
  transfers between devices with their start and end apart: 9 -> 9, of which waited for: 4 -> 5; matrix products, arithmetic and copies ran while one was open for 9% -> 1% of each run, Pallas kernels for 28% -> 4%
where the time goes in v2:
time: 102 us; the launch traced here: 100 us
  waiting for transfers between devices  37.6 us (37%)
  Pallas kernels  29.4 us (29%)
  starting transfers between devices  29.3 us (29%)
  local copies, waits for them, and re-layouts  1.93 us (2%)
  between operations  1.37 us (1%)
    ppermute x1, waiting for transfers between devices, body(): lax.ppermute(last_rows, 'gy', ring(along, 1))  25.1 us
    all_to_all x1, starting transfers between devices, body(): lax.all_to_all(message.reshape(devices, SLOTS, 8, 128), ('gx', 'gy'), spl...  11.5 us
    pallas_call x1, Pallas kernels, bin_blocks(): pl.pallas_call(bin_kernel, out_shape=(shape(height + 1, 8, width), shape(...  10.8 us
    pallas_call x1, Pallas kernels, smooth(): pl.pallas_call(smooth_kernel, out_shape=(jax.ShapeDtypeStruct((6, height,...  8.85 us
    ppermute x1, waiting for transfers between devices, body(): lax.ppermute(last_cols, 'gx', ring(across, 1))  6.38 us
    pallas_call x1, Pallas kernels, pack(): pl.pallas_call(pack_kernel, out_shape=(jax.ShapeDtypeStruct((devices * SL...  5.71 us
    ppermute x1, starting transfers between devices, body(): east = lax.ppermute(near, 'gx', ring(across, -1))  5.34 us
    ppermute x1, starting transfers between devices, body(): lax.ppermute(first_cols, 'gx', ring(across, -1))  4.27 us
  transfers between devices with their start and end apart: 9, of which 5 were waited for; matrix products, arithmetic and copies ran while one was open for 1% of the time, Pallas kernels for 4%

profile of v2, /device:TPU:0, one launch (start us, length us, event | category | flops | bytes accessed | tf_op | source)
XLA Modules:
  0.0 100.3 jit_solution(15457087303850626864)
XLA Ops:
  1.3 5.7 %pack.1 = (bf16[1664,8,128]{2,1,0:T(8,128)(2,1)}, f32[8,128]{1,0:T(8,128)}) custom-call(s32[1]{0:T(128)S(6)} %copy.10.count_ref, s32[1,1024]{1,0:T(1,128)} %bitcast.12, s32[1,1024]{1,0:T(1,128)} %bitcast.13, bf16[6,1024,128]{2,1,0:T(8,128)(2,1)} %bitcast.11, bf16[1024,128]{1,0:T(8,128)(2,1)} %weight_ref.1, s32[1024,128]{1,0:T(8,128)} %cols_ref.1), custom_call_target="tpu_custom_call" | custom-call | tf_op jit(solution)/shard_map/pack/pallas_call | solution.py:123
  7.0 11.5 %all-to-all-start = ((bf16[128,13,8,128]{3,2,1,0:T(8,128)(2,1)}), bf16[128,13,8,128]{3,2,1,0:T(8,128)(2,1)S(1)}, u32[]{:S(2)}, u32[]{:S(2)}) async-start(bf16[128,13,8,128]{3,2,1,0:T(8,128)(2,1)} %bitcast.10), calls=%async_computation | async-start | bytes 6815744 | tf_op jit(solution)/shard_map/all_to_all | solution.py:470
  18.5 1.8 %coefficient_edges.1 = (f32[2,256]{1,0:T(2,128)}, f32[2,256]{1,0:T(2,128)}, f32[2,256]{1,0:T(2,128)}, f32[2,256]{1,0:T(2,128)}) custom-call(f32[8,128]{1,0:T(8,128)} %get-tuple-element.17.after_ref, f32[256,256]{1,0:T(8,128)} %cx_ref.3, f32[256,256]{1,0:T(8,128)} %cy_ref.3), custom_call_target="tpu_custom_call" | custom-call | tf_op jit(solution)/shard_map/coefficient_edges/pallas_call | solution.py:410
  20.3 0.0 collective-permute-start
  20.4 3.0 %collective-permute-start.1 = (f32[2,256]{1,0:T(2,128)}, f32[2,256]{1,0:T(2,128)S(1)}, u32[]{:S(2)}, u32[]{:S(2)}) collective-permute-start(f32[2,256]{1,0:T(2,128)} %get-tuple-element.19), channel_id=1, source_target_pairs={{0,7},{1,0},{2,1},{3,2},{4,3},{5,4},{6,5},{7,6},{8,15},{9,8},{10,9... | collective-permute-start | bytes 6152 | tf_op jit(solution)/shard_map/ppermute | solution.py:484
  23.3 1.1 %collective-permute-start.2 = (f32[2,256]{1,0:T(2,128)}, f32[2,256]{1,0:T(2,128)S(1)}, u32[]{:S(2)}, u32[]{:S(2)}) collective-permute-start(f32[2,256]{1,0:T(2,128)} %get-tuple-element.20), channel_id=1, source_target_pairs={{0,8},{8,16},{16,24},{24,32},{32,40},{40,48},{48,56},{56,64},{64,7... | collective-permute-start | bytes 6152 | tf_op jit(solution)/shard_map/ppermute | solution.py:485
  24.4 4.3 %collective-permute-start.3 = (f32[2,256]{1,0:T(2,128)}, f32[2,256]{1,0:T(2,128)S(1)}, u32[]{:S(2)}, u32[]{:S(2)}) collective-permute-start(f32[2,256]{1,0:T(2,128)} %get-tuple-element.21), channel_id=1, source_target_pairs={{0,120},{8,0},{16,8},{24,16},{32,24},{40,32},{48,40},{56,48},{64,5... | collective-permute-start | bytes 6152 | tf_op jit(solution)/shard_map/ppermute | solution.py:486
  28.7 0.7 add_convert_fusion.flags_ref
  29.3 0.0 copy-start.2
  29.3 25.1 %collective-permute-done.up_ref = f32[2,256]{1,0:T(2,128)S(1)} collective-permute-done((f32[2,256]{1,0:T(2,128)}, f32[2,256]{1,0:T(2,128)S(1)}, u32[]{:S(2)}, u32[]{:S(2)}) %collective-permute-start) | collective-permute-done | bytes 2080 | tf_op jit(solution)/shard_map/ppermute | solution.py:483
  54.4 0.0 copy-start.4
  54.4 0.0 collective-permute-done.1.down_ref
  54.4 0.0 copy-start.5
  54.4 6.4 %collective-permute-done.2.west_ref = f32[2,256]{1,0:T(2,128)S(1)} collective-permute-done((f32[2,256]{1,0:T(2,128)}, f32[2,256]{1,0:T(2,128)S(1)}, u32[]{:S(2)}, u32[]{:S(2)}) %collective-permute-start.2) | collective-permute-done | bytes 2080 | tf_op jit(solution)/shard_map/ppermute | solution.py:485
  60.8 0.0 copy-start.6
  60.8 0.0 collective-permute-done.3.east_ref
  60.8 0.0 copy-done.4
  60.8 0.0 copy-done.5
  60.8 0.6 copy-done.6
  61.4 0.0 copy-start.7
  61.4 0.6 copy-done.7
  61.9 2.1 %extend.1 = (f32[258,384]{1,0:T(8,128)}, f32[258,384]{1,0:T(8,128)}, f32[8,128]{1,0:T(8,128)}) custom-call(s32[4]{0:T(128)} %add_convert_fusion.flags_ref, f32[256,256]{1,0:T(8,128)} %cx_ref.3, f32[256,256]{1,0:T(8,128)} %cy_ref.3, f32[2,256]{1,0:T(2,128)} %copy-done.4, f32[2,256]{1,0:T(2,128)} %copy-done.5, f32[2,256]{1,0:T(2,128)} %copy-done.6, ...), custom_call_target="tpu_custom_call" | custom-call | tf_op jit(solution)/shard_map/extend/pallas_call | solution.py:445
  64.1 0.0 all-to-all-done
  64.1 0.0 copy-start
  64.1 0.0 copy-start.1
  64.1 0.0 copy-start.3
  64.1 0.8 copy-done.3
  64.8 10.8 %bin.1 = (f32[257,8,256]{2,1,0:T(8,128)S(1)}, f32[2,8,256]{2,1,0:T(8,128)S(1)}, f32[2,8,256]{2,1,0:T(8,128)S(1)}, f32[4,8,128]{2,1,0:T(8,128)S(1)}, f32[4,8,128]{2,1,0:T(8,128)S(1)}) custom-call(bf16[1664,8,128]{2,1,0:T(8,128)(2,1)S(1)} %bitcast.9, f32[8,128]{1,0:T(8,128)S(1)} %copy-done.3), custom_call_target="tpu_custom_call" | custom-call | tf_op jit(solution)/shard_map/bin/pallas_call | solution.py:265
  75.7 4.2 %collective-permute-start.5 = (f32[2,8,256]{2,1,0:T(8,128)S(1)}, f32[2,8,256]{2,1,0:T(8,128)S(1)}, u32[]{:S(2)}, u32[]{:S(2)}) collective-permute-start(f32[2,8,256]{2,1,0:T(8,128)S(1)} %get-tuple-element.25), channel_id=1, source_target_pairs={{0,7},{1,0},{2,1},{3,2},{4,3},{5,4},{6,5},{7,6},{8,15},{9,8},{10,9... | collective-permute-start | bytes 49160 | tf_op jit(solution)/shard_map/ppermute | solution.py:491
  79.9 0.0 collective-permute-start.4
  79.9 1.4 %collective-permute-done.5.down_ref = f32[2,8,256]{2,1,0:T(8,128)S(1)} collective-permute-done((f32[2,8,256]{2,1,0:T(8,128)S(1)}, f32[2,8,256]{2,1,0:T(8,128)S(1)}, u32[]{:S(2)}, u32[]{:S(2)}) %collective-permute-start.5) | collective-permute-done | bytes 16416 | tf_op jit(solution)/shard_map/ppermute | solution.py:491
  81.3 2.9 %collective-permute-done.4.up_ref = f32[2,8,256]{2,1,0:T(8,128)S(1)} collective-permute-done((f32[2,8,256]{2,1,0:T(8,128)S(1)}, f32[2,8,256]{2,1,0:T(8,128)S(1)}, u32[]{:S(2)}, u32[]{:S(2)}) %collective-permute-start.4) | collective-permute-done | bytes 16416 | tf_op jit(solution)/shard_map/ppermute | solution.py:490
  84.3 0.0 collective-permute-start.6
  84.3 5.3 %collective-permute-start.7 = (f32[6,8,128]{2,1,0:T(8,128)S(1)}, f32[6,8,128]{2,1,0:T(8,128)S(1)}, u32[]{:S(2)}, u32[]{:S(2)}) collective-permute-start(f32[6,8,128]{2,1,0:T(8,128)S(1)} %pad_maximum_fusion.1), channel_id=1, source_target_pairs={{0,120},{8,0},{16,8},{24,16},{32,24},{40,32},{48,40},{56,48},{64,5... | collective-permute-start | bytes 73736 | tf_op jit(solution)/shard_map/ppermute | solution.py:495
  89.6 1.8 %collective-permute-done.6.west_ref = f32[6,8,128]{2,1,0:T(8,128)S(1)} collective-permute-done((f32[6,8,128]{2,1,0:T(8,128)S(1)}, f32[6,8,128]{2,1,0:T(8,128)S(1)}, u32[]{:S(2)}, u32[]{:S(2)}) %collective-permute-start.6) | collective-permute-done | bytes 24608 | tf_op jit(solution)/shard_map/ppermute | solution.py:494
  91.4 0.0 collective-permute-done.7.east_ref
  91.4 0.0 copy-done.2
  91.4 0.0 copy-done
  91.4 0.0 copy-done.1
  91.4 8.9 %smooth.1 = (f32[6,256,256]{2,1,0:T(8,128)}, f32[256,256]{1,0:T(8,128)}) custom-call(s32[4]{0:T(128)S(1)} %copy-done.2, f32[257,8,256]{2,1,0:T(8,128)S(1)} %get-tuple-element.23.acc_ref, f32[2,8,256]{2,1,0:T(8,128)S(1)} %collective-permute-done.4.up_ref, f32[2,8,256]{2,1,0:T(8,128)S(1)} %collective-permute-done.5.down_ref, ...), custom_call_target="tpu_custom_call" | custom-call | tf_op jit(solution)/shard_map/smooth/pallas_call | solution.py:378
  (4 shorter events, 0.0 us)
Async XLA Ops:
  7.0 57.1 %all-to-all-start = ((bf16[128,13,8,128]{3,2,1,0:T(8,128)(2,1)}), bf16[128,13,8,128]{3,2,1,0:T(8,128)(2,1)S(1)}, u32[]{:S(2)}, u32[]{:S(2)}) async-start(bf16[128,13,8,128]{3,2,1,0:T(8,128)(2,1)} %bitcast.10), calls=%async_computation | async-start | bytes 6815744 | tf_op jit(solution)/shard_map/all_to_all | solution.py:470
  20.3 34.0 %collective-permute-start = (f32[2,256]{1,0:T(2,128)}, f32[2,256]{1,0:T(2,128)S(1)}, u32[]{:S(2)}, u32[]{:S(2)}) collective-permute-start(f32[2,256]{1,0:T(2,128)} %get-tuple-element.18), channel_id=1, source_target_pairs={{0,1},{1,2},{2,3},{3,4},{4,5},{5,6},{6,7},{7,0},{8,9},{9,10},{10,1... | collective-permute-start | bytes 6152 | tf_op jit(solution)/shard_map/ppermute | solution.py:483
  20.4 34.0 %collective-permute-start.1 = (f32[2,256]{1,0:T(2,128)}, f32[2,256]{1,0:T(2,128)S(1)}, u32[]{:S(2)}, u32[]{:S(2)}) collective-permute-start(f32[2,256]{1,0:T(2,128)} %get-tuple-element.19), channel_id=1, source_target_pairs={{0,7},{1,0},{2,1},{3,2},{4,3},{5,4},{6,5},{7,6},{8,15},{9,8},{10,9... | collective-permute-start | bytes 6152 | tf_op jit(solution)/shard_map/ppermute | solution.py:484
  23.3 37.5 %collective-permute-start.2 = (f32[2,256]{1,0:T(2,128)}, f32[2,256]{1,0:T(2,128)S(1)}, u32[]{:S(2)}, u32[]{:S(2)}) collective-permute-start(f32[2,256]{1,0:T(2,128)} %get-tuple-element.20), channel_id=1, source_target_pairs={{0,8},{8,16},{16,24},{24,32},{32,40},{40,48},{48,56},{56,64},{64,7... | collective-permute-start | bytes 6152 | tf_op jit(solution)/shard_map/ppermute | solution.py:485
  24.4 36.4 %collective-permute-start.3 = (f32[2,256]{1,0:T(2,128)}, f32[2,256]{1,0:T(2,128)S(1)}, u32[]{:S(2)}, u32[]{:S(2)}) collective-permute-start(f32[2,256]{1,0:T(2,128)} %get-tuple-element.21), channel_id=1, source_target_pairs={{0,120},{8,0},{16,8},{24,16},{32,24},{40,32},{48,40},{56,48},{64,5... | collective-permute-start | bytes 6152 | tf_op jit(solution)/shard_map/ppermute | solution.py:486
  29.3 62.1 %copy-start.2 = (s32[4]{0:T(128)S(1)}, s32[4]{0:T(128)}, u32[]{:S(2)}) copy-start(s32[4]{0:T(128)} %add_convert_fusion.flags_ref) | copy-start | bytes 52
  54.4 6.4 %copy-start.4 = (f32[2,256]{1,0:T(2,128)}, f32[2,256]{1,0:T(2,128)S(1)}, u32[]{:S(2)}) copy-start(f32[2,256]{1,0:T(2,128)S(1)} %collective-permute-done.up_ref) | copy-start | bytes 6148
  54.4 6.4 %copy-start.5 = (f32[2,256]{1,0:T(2,128)}, f32[2,256]{1,0:T(2,128)S(1)}, u32[]{:S(2)}) copy-start(f32[2,256]{1,0:T(2,128)S(1)} %collective-permute-done.1.down_ref) | copy-start | bytes 6148
  60.8 0.6 copy-start.6
  61.4 0.6 copy-start.7
  64.1 27.3 %copy-start = (f32[258,384]{1,0:T(8,128)S(1)}, f32[258,384]{1,0:T(8,128)}, u32[]{:S(2)}) copy-start(f32[258,384]{1,0:T(8,128)} %get-tuple-element.28.cx_ref) | copy-start | bytes 1188868
  64.1 27.3 %copy-start.1 = (f32[258,384]{1,0:T(8,128)S(1)}, f32[258,384]{1,0:T(8,128)}, u32[]{:S(2)}) copy-start(f32[258,384]{1,0:T(8,128)} %get-tuple-element.29.cy_ref) | copy-start | bytes 1188868
  64.1 0.8 copy-start.3
  75.7 5.6 %collective-permute-start.5 = (f32[2,8,256]{2,1,0:T(8,128)S(1)}, f32[2,8,256]{2,1,0:T(8,128)S(1)}, u32[]{:S(2)}, u32[]{:S(2)}) collective-permute-start(f32[2,8,256]{2,1,0:T(8,128)S(1)} %get-tuple-element.25), channel_id=1, source_target_pairs={{0,7},{1,0},{2,1},{3,2},{4,3},{5,4},{6,5},{7,6},{8,15},{9,8},{10,9... | collective-permute-start | bytes 49160 | tf_op jit(solution)/shard_map/ppermute | solution.py:491
  79.9 4.4 %collective-permute-start.4 = (f32[2,8,256]{2,1,0:T(8,128)S(1)}, f32[2,8,256]{2,1,0:T(8,128)S(1)}, u32[]{:S(2)}, u32[]{:S(2)}) collective-permute-start(f32[2,8,256]{2,1,0:T(8,128)S(1)} %get-tuple-element.24), channel_id=1, source_target_pairs={{0,1},{1,2},{2,3},{3,4},{4,5},{5,6},{6,7},{7,0},{8,9},{9,10},{10,1... | collective-permute-start | bytes 49160 | tf_op jit(solution)/shard_map/ppermute | solution.py:490
  84.3 7.1 %collective-permute-start.6 = (f32[6,8,128]{2,1,0:T(8,128)S(1)}, f32[6,8,128]{2,1,0:T(8,128)S(1)}, u32[]{:S(2)}, u32[]{:S(2)}) collective-permute-start(f32[6,8,128]{2,1,0:T(8,128)S(1)} %pad_maximum_fusion), channel_id=1, source_target_pairs={{0,8},{8,16},{16,24},{24,32},{32,40},{40,48},{48,56},{56,64},{64,7... | collective-permute-start | bytes 73736 | tf_op jit(solution)/shard_map/ppermute | solution.py:494
  84.3 7.1 %collective-permute-start.7 = (f32[6,8,128]{2,1,0:T(8,128)S(1)}, f32[6,8,128]{2,1,0:T(8,128)S(1)}, u32[]{:S(2)}, u32[]{:S(2)}) collective-permute-start(f32[6,8,128]{2,1,0:T(8,128)S(1)} %pad_maximum_fusion.1), channel_id=1, source_target_pairs={{0,120},{8,0},{16,8},{24,16},{32,24},{40,32},{48,40},{56,48},{64,5... | collective-permute-start | bytes 73736 | tf_op jit(solution)/shard_map/ppermute | solution.py:495
